TPU v7x, 512 devices: a whole 4x4x16 slice. The times are simulated.
512 devices in a mesh: hst: 32 (over y, x, core), tp: 16 (over z).
Axes of the slice: x: 4, y: 4, z: 16, core: 2. Of those that a mesh axis runs over, the one named last changes fastest.
Arguments:
- ctx_q: bfloat16 [24576, 8192], P('hst', 'tp'), may hold values from -11.2 to 11.2
- ctx_kv: bfloat16 [2, 24576, 1024], P(None, 'hst'), may hold values from -4.5 to 4.5
- lengths: int32 [32], replicated, may hold values from 192 to 768, as said below
- query_q: bfloat16 [64, 8192], P('hst', 'tp'), may hold values from -11.2 to 11.2
- query_kv: bfloat16 [2, 64, 1024], P(None, 'hst'), may hold values from -4.5 to 4.5
- out_weight: bfloat16 [8192, 8192], P('tp', 'hst'), may hold values from -0.0625 to 0.0625
Outputs:
- context_out: bfloat16 [24576, 8192], P('hst', 'tp')
- query_out: bfloat16 [64, 8192], P(None, 'hst')
Inputs may be any that keep to these rules, and one draw needn't show every extreme that they name: lengths[0] is 768; blocks with index below three quarters of 32 are full, the last block holds 192 live positions.
All inputs are finite; a program needn't handle non-finite values.
Results may differ from a plain program's by a relative error of at most 0.012.
Values may be sent and summed in bfloat16 or wider, within the bound.
A program may use at most 64 MiB of HBM per device.

v0:
```python
import jax
import jax.numpy as jnp
from jax import lax
from jax.sharding import PartitionSpec as P

H = 64
KVH = 8
HD = 128


MASKED = -1e30


def spread(value, axis, source):
    kept = jnp.where(lax.axis_index(axis) == source, value, 0).astype(value.dtype)
    return lax.psum(kept, axis)


def softmax_rows(query_rows, key_rows, allowed, score_scale):
    scores = (
        jnp.einsum("id,jd->ij", query_rows, key_rows, preferred_element_type=jnp.float32)
        * score_scale
    )
    scores = jnp.where(allowed, scores, MASKED)
    return scores


def per_device(ctx_q, ctx_kv, lengths, query_q, query_kv, out_weight):
    slab_rows = ctx_q.shape[0]
    local_heads = ctx_q.shape[1] // HD
    group_size = H // KVH
    kv_local = max(1, local_heads // group_size)
    per_kv = min(local_heads, group_size)
    score_scale = HD ** (-0.5)
    tp_index = lax.axis_index("tp")
    host_id = lax.axis_index("hst")
    kv_first = tp_index * local_heads // group_size
    own_kv = lax.dynamic_slice_in_dim(ctx_kv, kv_first * HD, kv_local * HD, 2)
    anchor = spread(own_kv, "hst", 0)
    own_len = lengths[host_id]
    first_len = lengths[0]
    row_ids = jnp.arange(slab_rows)
    own_ok = (row_ids[None, :] <= row_ids[:, None]) & (row_ids[None, :] < own_len)
    anchor_ok = (row_ids[None, :] < first_len) & (host_id > 0)
    allowed = jnp.concatenate([jnp.broadcast_to(anchor_ok, (slab_rows, slab_rows)), own_ok], 1)
    joined = jnp.concatenate([anchor, own_kv], 1)
    joined = joined.reshape(2, 2 * slab_rows, kv_local, HD).transpose(0, 2, 1, 3)
    head_queries = ctx_q.reshape(slab_rows, local_heads, HD).transpose(1, 0, 2)

    def encode_head(operands):
        query_rows, head_index = operands
        kv_index = head_index // per_kv
        scores = softmax_rows(query_rows, joined[0, kv_index], allowed, score_scale)
        peak = jnp.max(scores, axis=1, keepdims=True)
        expo = jnp.exp(scores - peak)
        probs = (expo / jnp.sum(expo, axis=1, keepdims=True)).astype(jnp.bfloat16)
        encoded = jnp.einsum(
            "ij,jd->id", probs, joined[1, kv_index], preferred_element_type=jnp.float32
        )
        return encoded.astype(jnp.bfloat16)

    encoded = lax.map(encode_head, (head_queries, jnp.arange(local_heads)))
    encoded = encoded.transpose(1, 0, 2).reshape(slab_rows, local_heads * HD)
    context_out = jnp.where((row_ids < own_len)[:, None], encoded, jnp.zeros_like(encoded))
    all_queries = lax.all_gather(query_q, "hst", axis=0, tiled=True)
    query_count = all_queries.shape[0]
    q_rows = query_q.shape[0]
    self_kv = lax.dynamic_slice_in_dim(query_kv, kv_first * HD, kv_local * HD, 2)
    source = jnp.concatenate([own_kv, self_kv], 1)
    source = source.reshape(2, slab_rows + q_rows, kv_local, HD).transpose(0, 2, 1, 3)
    query_ids = jnp.arange(query_count)
    context_ok = jnp.broadcast_to(row_ids[None, :] < own_len, (query_count, slab_rows))
    self_ok = (host_id * q_rows + jnp.arange(q_rows))[None, :] <= query_ids[:, None]
    seen_ok = jnp.concatenate([context_ok, self_ok], 1)
    query_heads = all_queries.reshape(query_count, local_heads, HD).transpose(1, 0, 2)

    def score_head(operands):
        query_rows, head_index = operands
        kv_index = head_index // per_kv
        scores = softmax_rows(query_rows, source[0, kv_index], seen_ok, score_scale)
        peak = jnp.max(scores, axis=1)
        expo = jnp.exp(scores - peak[:, None])
        denominator = jnp.sum(expo, axis=1)
        weighted = jnp.einsum(
            "ij,jd->id",
            expo.astype(jnp.bfloat16),
            source[1, kv_index],
            preferred_element_type=jnp.float32,
        )
        return (peak, denominator, weighted)

    maxima, totals, outputs = lax.map(score_head, (query_heads, jnp.arange(local_heads)))
    highest = lax.pmax(maxima, "hst")
    factor = jnp.exp(maxima - highest)
    denominator, summed = lax.psum((totals * factor, outputs * factor[..., None]), "hst")
    attended = (summed / denominator[..., None]).astype(jnp.bfloat16)
    attended = attended.transpose(1, 0, 2).reshape(query_count, local_heads * HD)
    partial_out = jnp.dot(attended, out_weight, preferred_element_type=jnp.float32)
    query_out = lax.psum(partial_out, "tp").astype(jnp.bfloat16)
    return (context_out, query_out)


def solution(mesh):
    return jax.shard_map(
        per_device,
        mesh=mesh,
        in_specs=(
            P("hst", "tp"),
            P(None, "hst", None),
            P(),
            P("hst", "tp"),
            P(None, "hst", None),
            P("tp", "hst"),
        ),
        out_specs=(P("hst", "tp"), P(None, "hst")),
        check_vma=False,
    )
```

profile of v0, /device:TPU:1, one launch (start us, length us, event | category | flops | bytes accessed | tf_op | source)
XLA Modules:
  0.0 398.9 jit_solution(9686451060329737219)
XLA Ops:
  7.3 1.3 fusion.34
  8.6 0.6 iota_compare_fusion.3
  9.3 28.5 %all-gather = bf16[32,2,512]{2,1,0:T(2,128)(2,1)S(1)} all-gather(bf16[1,2,512]{2,1,0:T(2,128)(2,1)} %bitcast.89), channel_id=1, replica_groups=mesh['hst'=32,'tp'=16] {'hst'}, dimensions={0}, use_global_device_ids=true | all-gather | bytes 67584 | tf_op jit(solution)/shard_map/all_gather | solution.py:65
  37.9 0.7 constant_dynamic-slice_fusion
  38.6 1.9 broadcast_select_fusion
  40.5 3.4 while.27
  40.5 0.3 fusion.54
  43.9 62.2 %pmax.7 = f32[4,64]{1,0:T(4,128)S(1)} all-reduce(f32[4,64]{1,0:T(4,128)S(1)} %get-tuple-element.102), channel_id=1, replica_groups=mesh['hst'=32,'tp'=16] {'hst'}, use_global_device_ids=true, to_apply=%region_9.10 | all-reduce | flops 256 | bytes 2048 | tf_op jit(solution)/shard_map/pmax | solution.py:93
  106.1 0.8 broadcast_multiply_fusion
  107.0 0.7 all-reduce.3.cloned.1.call-update
  107.8 65.3 %psum.30 = f32[4,64]{1,0:T(4,128)S(1)} all-reduce(f32[4,64]{1,0:T(4,128)S(1)} %get-tuple-element.157), channel_id=1, replica_groups=mesh['hst'=32,'tp'=16] {'hst'}, use_global_device_ids=true, to_apply=%region_11.12 | all-reduce | flops 256 | bytes 2048 | tf_op jit(solution)/shard_map/psum | solution.py:95
  173.1 0.7 fusion.30
  174.1 0.5 pad_add_fusion
  174.5 62.3 %all-reduce.5.cloned.1.call-done = f32[4,64,128]{2,1,0:T(8,128)} async-done(((f32[4,64,128]{2,1,0:T(8,128)}), f32[4,64,128]{2,1,0:T(8,128)}) %all-reduce.5.cloned.1.call-update) | async-done | bytes 131088 | tf_op jit(solution)/shard_map/psum | solution.py:95
  236.8 1.1 fusion.26
  237.9 45.0 %psum.31 = bf16[64,256]{1,0:T(8,128)(2,1)} all-reduce(f32[64,256]{1,0:T(8,128)S(1)} %fusion.26), channel_id=1, replica_groups=mesh['hst'=32,'tp'=16] {'tp'}, use_global_device_ids=true, to_apply=%region_12.13 | all-reduce | flops 16384 | bytes 98304 | tf_op jit(solution)/shard_map/psum | solution.py:99
  283.0 91.2 %all-reduce.3.cloned.1.call-done = bf16[2,768,128]{2,1,0:T(8,128)(2,1)} async-done(((bf16[2,768,128]{2,1,0:T(8,128)(2,1)}), bf16[2,768,128]{2,1,0:T(8,128)(2,1)}) %all-reduce.3.cloned.1.call-update) | async-done | bytes 393232 | tf_op jit(solution)/shard_map/psum | solution.py:16
  374.2 1.0 maximum_bitcast_fusion
  375.3 14.5 %while.26 = (s32[]{:T(128)}, bf16[4,768,128]{2,1,0:T(8,128)(2,1)}, bf16[4,768,128]{1,2,0:T(8,128)(2,1)S(1)}, bf16[2,1,1536,128]{3,2,1,0:T(8,128)(2,1)S(1)}, pred[768,1536]{1,0:T(32,128)(4,1)S(1)}, /*index=5*/s32[]{:T(128)}) while((s32[]{:T(128)}, bf16[4,768,128]{2,1,0:T(8,128)(2,1)}, bf16[4,768,128]{1,2,0:T(8,128)(2,1)S(1)}, ...), condition=%wide.region_4.5_spmd, body=%wide.region_1.4_spmd.sunk | while | flops 613513728 | bytes 16533065 | solution.py:62
  375.3 1.2 fusion.49
  376.5 0.8 fusion.50
  377.3 1.7 fusion.51
  378.9 1.2 fusion.49
  380.1 0.8 fusion.50
  380.9 1.7 fusion.51
  382.5 1.2 fusion.49
  383.7 0.8 fusion.50
  384.5 1.7 fusion.51
  386.2 1.2 fusion.49
  387.4 0.8 fusion.50
  388.1 1.7 fusion.51
  389.8 2.3 bitcast_select_fusion
  (41 shorter events, 3.7 us)
Async XLA Ops:
  7.2 229.7 %copy-start = (bf16[512,256]{1,0:T(8,128)(2,1)S(1)}, bf16[512,256]{1,0:T(8,128)(2,1)}, u32[]{:S(2)}) copy-start(bf16[512,256]{1,0:T(8,128)(2,1)} %param.15) | copy-start | bytes 786436
  7.2 229.6 %all-reduce.5.cloned.1.call-start = ((), (), s32[]{:S(2)}) async-start(), calls=%async_computation.1 | async-start | bytes 262144 | tf_op jit(solution)/shard_map/psum | solution.py:95
  40.5 133.3 %copy-start.1 = (bf16[768,512]{1,0:T(8,128)(2,1)S(1)}, bf16[768,512]{1,0:T(8,128)(2,1)}, u32[]{:S(2)}) copy-start(bf16[768,512]{1,0:T(8,128)(2,1)} %param.10) | copy-start | bytes 2359300
  106.9 267.3 %all-reduce.3.cloned.1.call-start = ((), (), s32[]{:S(2)}) async-start(), calls=%async_computation | async-start | bytes 786432 | tf_op jit(solution)/shard_map/psum | solution.py:16
Sparse Core Ops, SparseCore 0:
  107.0 129.7 all-reduce.4
  240.9 133.2 all-reduce.2
where the time goes:
time: 399 us
  blocking collectives  201 us (50%)
  waiting for transfers between devices  154 us (39%)
  matrix products  14.7 us (4%)
  between operations  14.2 us (4%)
  other arithmetic  11.8 us (3%)
    psum x1, waiting for transfers between devices, spread(): return lax.psum(kept, axis)  91.2 us
    psum x1, blocking collectives, per_device(): lax.psum((totals * factor, outputs * factor[..., None]), 'hst')  65.3 us
    psum x1, waiting for transfers between devices, per_device(): lax.psum((totals * factor, outputs * factor[..., None]), 'hst')  62.3 us
    pmax x1, blocking collectives, per_device(): highest = lax.pmax(maxima, 'hst')  62.2 us
    psum x1, blocking collectives, per_device(): query_out = lax.psum(partial_out, 'tp').astype(jnp.bfloat16)  45 us
    all_gather x1, blocking collectives, per_device(): all_queries = lax.all_gather(query_q, 'hst', axis=0, tiled=True)  28.5 us
  transfers between devices with their start and end apart: 2, of which 2 were waited for; matrix products, arithmetic and copies ran while one was open for 1% of the time, Pallas kernels for 0%

commit v1 on v0

v1 whole, which is shorter than its diff:
```python
import jax
import jax.numpy as jnp
from jax import lax
from jax.experimental import pallas as pl
from jax.experimental.pallas import tpu as pltpu
from jax.sharding import PartitionSpec as P

H = 64
KVH = 8
HD = 128
HST = 32
TP = 16
ROWS = 768
HEADS = H // TP
TILE = 256
CHIPS = HST // 2
PIECE = ROWS // CHIPS
QN = 64
COLS = 256
MASKED = -1e30
SCALE2 = HD ** (-0.5) * 1.4426950408889634
MESH = pl.DeviceIdType.MESH


def dot_t(a, b):
    return lax.dot_general(a, b, (((1,), (1,)), ((), ())), preferred_element_type=jnp.float32)


def dot(a, b):
    return jnp.dot(a, b, preferred_element_type=jnp.float32)


def with_ones(values):
    return jnp.concatenate([values, jnp.ones_like(values)], axis=1)


def kernel(
    lengths,
    ctx_q,
    ctx_kv,
    query_q,
    query_kv,
    out_weight,
    ctx_out,
    query_out,
    cq,
    own,
    anchor,
    weight,
    qq,
    qkv,
    selfkv,
    out1,
    sum1,
    max1,
    enc,
    gather_q,
    rows_q,
    sent_b,
    got_b,
    att,
    part,
    got_d,
    got_e,
    qout,
    local_sem,
    out_sem,
    send_sem,
    recv_sem,
):
    me = lax.axis_index("hst")
    z = lax.axis_index("tp")
    chip = me // 2
    core = lax.rem(me, 2)
    kv_off = pl.multiple_of((z // 2) * HD, HD)

    def at_hst(d):
        return {"hst": d}

    def at_tp(d):
        return {"tp": d}

    load_kv = pltpu.make_async_copy(ctx_kv.at[:, :, pl.ds(kv_off, HD)], own, local_sem.at[0])
    load_cq = pltpu.make_async_copy(ctx_q, cq, local_sem.at[1])
    load_qq = pltpu.make_async_copy(query_q, qq, local_sem.at[2])
    load_qkv = pltpu.make_async_copy(query_kv, qkv, local_sem.at[3])
    load_w = pltpu.make_async_copy(out_weight, weight, local_sem.at[4])
    for copy in (load_qq, load_kv, load_cq, load_qkv, load_w):
        copy.start()

    barrier = pltpu.get_barrier_semaphore()

    @pl.loop(1, HST)
    def _(k):
        pl.semaphore_signal(
            barrier, inc=1, device_id=at_hst(lax.rem(me + k, HST)), device_id_type=MESH
        )

    @pl.loop(1, TP)
    def _(k):
        pl.semaphore_signal(
            barrier, inc=1, device_id=at_tp(lax.rem(z + k, TP)), device_id_type=MESH
        )

    own_len = lengths[me]

    diag_row = lax.broadcasted_iota(jnp.int32, (TILE, TILE), 0)
    diag_col = lax.broadcasted_iota(jnp.int32, (TILE, TILE), 1)

    def own_head(h):
        for rb in range(ROWS // TILE):
            rows = pl.ds(rb * TILE, TILE)
            q = cq[rows, h * HD : (h + 1) * HD]
            keys = (rb + 1) * TILE
            s = dot_t(q, own[0, 0:keys, :])
            last = jnp.where(diag_col <= diag_row, s[:, keys - TILE :], MASKED)
            s = last if rb == 0 else jnp.concatenate([s[:, : keys - TILE], last], axis=1)
            m = jnp.max(s, axis=1, keepdims=True) * SCALE2
            p = jnp.exp2(s * SCALE2 - m).astype(jnp.bfloat16)
            o = dot(p, with_ones(own[1, 0:keys, :]))
            out1[h, rows, :] = o[:, :HD]
            sum1[h, rows, :] = o[:, HD:]
            max1[h, rows, :] = jnp.broadcast_to(m, (TILE, HD))

    def live(rb, value):
        rid = rb * TILE + lax.broadcasted_iota(jnp.int32, (TILE, HD), 0)
        return jnp.where(rid < own_len, value, 0.0).astype(jnp.bfloat16)

    def anchor_head(h):
        for rb in range(ROWS // TILE):
            rows = pl.ds(rb * TILE, TILE)
            q = cq[rows, h * HD : (h + 1) * HD]
            s = dot_t(q, anchor[0])
            before = max1[h, rows, :]
            m = jnp.maximum(jnp.max(s, axis=1, keepdims=True) * SCALE2, before[:, :1])
            p = jnp.exp2(s * SCALE2 - m).astype(jnp.bfloat16)
            o = dot(p, with_ones(anchor[1]))
            keep = jnp.exp2(before - m)
            num = out1[h, rows, :] * keep + o[:, :HD]
            den = sum1[h, rows, :] * keep + o[:, HD:]
            enc[rows, h * HD : (h + 1) * HD] = live(rb, num / den)

    def first_head(h):
        for rb in range(ROWS // TILE):
            rows = pl.ds(rb * TILE, TILE)
            enc[rows, h * HD : (h + 1) * HD] = live(rb, out1[h, rows, :] / sum1[h, rows, :])

    def finish_head(h):
        @pl.when(me > 0)
        def _():
            anchor_head(h)

        @pl.when(me == 0)
        def _():
            first_head(h)

        pltpu.make_async_copy(
            enc.at[:, pl.ds(h * HD, HD)], ctx_out.at[:, pl.ds(h * HD, HD)], out_sem.at[h]
        ).start()

    load_qq.wait()
    mine = qq[...].astype(jnp.float32)
    gather_q[pl.ds(me, 1)] = jnp.concatenate(
        [mine[t : t + 1, h * HD : (h + 1) * HD] for t in range(2) for h in range(HEADS)], axis=0
    ).astype(jnp.bfloat16)[None]

    load_kv.wait()
    load_cq.wait()
    own_head(0)

    pl.semaphore_wait(barrier, HST - 1 + TP - 1)

    @pl.loop(1, HST)
    def _(k):
        pltpu.make_async_remote_copy(
            gather_q.at[me], gather_q.at[me], send_sem.at[0], recv_sem.at[0],
            device_id=at_hst(lax.rem(me + k, HST)), device_id_type=MESH,
        ).start()

    def piece(ref, plane, c):
        return ref.at[plane, pl.ds(pl.multiple_of(c * PIECE, 16), PIECE), :]

    @pl.when(me == 0)
    def _():
        @pl.loop(1, CHIPS)
        def _(c):
            pltpu.make_async_remote_copy(
                piece(own, 0, c), piece(anchor, 0, c), send_sem.at[1], recv_sem.at[1],
                device_id=at_hst(c * 2), device_id_type=MESH,
            ).start()
            pltpu.make_async_remote_copy(
                piece(own, 1, c), piece(anchor, 1, c), send_sem.at[2], recv_sem.at[1],
                device_id=at_hst(c * 2 + 1), device_id_type=MESH,
            ).start()

        pltpu.make_async_remote_copy(
            piece(own, 1, 0), piece(anchor, 1, 0), send_sem.at[2], recv_sem.at[1],
            device_id=at_hst(1), device_id_type=MESH,
        ).start()

        @pl.loop(1, CHIPS)
        def _(c):
            pltpu.make_async_remote_copy(
                piece(own, 0, 0), piece(anchor, 0, 0), send_sem.at[3], recv_sem.at[2],
                device_id=at_hst(c * 2), device_id_type=MESH,
            ).start()

        pltpu.make_async_remote_copy(
            own.at[0], anchor.at[0], send_sem.at[4], recv_sem.at[3],
            device_id=at_hst(1), device_id_type=MESH,
        ).start()

    own_head(1)
    own_head(2)

    @pl.when(me > 0)
    def _():
        pltpu.make_async_copy(
            piece(anchor, 0, 0), piece(anchor, 0, 0), recv_sem.at[1]
        ).wait()

        @pl.loop(1, CHIPS)
        def _(k):
            c = lax.rem(chip + k, CHIPS)

            @pl.when(c * 2 + core > 0)
            def _():
                pltpu.make_async_remote_copy(
                    piece(anchor, core, chip), piece(anchor, core, chip),
                    send_sem.at[3], recv_sem.at[2],
                    device_id=at_hst(c * 2 + core), device_id_type=MESH,
                ).start()

    pltpu.make_async_copy(
        gather_q.at[pl.ds(0, HST - 1)], gather_q.at[pl.ds(0, HST - 1)], recv_sem.at[0]
    ).wait()
    rows_q[...] = gather_q[...].astype(jnp.float32).reshape(HST * 8, HD)
    q_all = jnp.concatenate(
        [rows_q[pl.ds(h, QN, stride=HEADS), :] for h in range(HEADS)], axis=0
    ).astype(jnp.bfloat16)
    load_qkv.wait()
    for plane in range(2):
        tiny = qkv[plane, :, pl.ds(kv_off, HD)].astype(jnp.float32)
        selfkv[plane] = jnp.concatenate(
            [tiny, jnp.zeros((HD - 2, HD), jnp.float32)], axis=0
        ).astype(jnp.bfloat16)
    s_ctx = dot_t(q_all, own[0])
    s_ctx = jnp.where(
        lax.broadcasted_iota(jnp.int32, s_ctx.shape, 1) < own_len, s_ctx, MASKED
    )
    s_self = dot_t(q_all, selfkv[0])
    token = lax.rem(lax.broadcasted_iota(jnp.int32, s_self.shape, 0), QN)
    key = lax.broadcasted_iota(jnp.int32, s_self.shape, 1)
    s_self = jnp.where((key < 2) & (me * 2 + key <= token), s_self, MASKED)
    peak = jnp.maximum(
        jnp.max(s_ctx, axis=1, keepdims=True), jnp.max(s_self, axis=1, keepdims=True)
    )
    peak = (peak * SCALE2).astype(jnp.bfloat16).astype(jnp.float32)
    p_ctx = jnp.exp2(s_ctx * SCALE2 - peak).astype(jnp.bfloat16)
    p_self = jnp.exp2(s_self * SCALE2 - peak).astype(jnp.bfloat16)
    o = dot(p_ctx, with_ones(own[1])) + dot(p_self, with_ones(selfkv[1]))
    lane = lax.broadcasted_iota(jnp.int32, (HEADS * QN, HD), 1)
    stats = jnp.where(lane < HD // 2, jnp.broadcast_to(peak, (HEADS * QN, HD)), o[:, HD:])
    sent_b[...] = jnp.concatenate(
        [o[:, :HD].reshape(HST, 8, HD), stats.reshape(HST, 8, HD)], axis=1
    ).astype(jnp.bfloat16)

    @pl.loop(1, HST)
    def _(k):
        d = lax.rem(me + k, HST)
        pltpu.make_async_remote_copy(
            sent_b.at[d], got_b.at[me], send_sem.at[5], recv_sem.at[4],
            device_id=at_hst(d), device_id_type=MESH,
        ).start()

    got_b[pl.ds(me, 1)] = sent_b[pl.ds(me, 1)]

    own_head(3)

    @pl.when(me > 0)
    def _():
        pltpu.make_async_copy(
            anchor.at[0, pl.ds(0, ROWS - PIECE)], anchor.at[0, pl.ds(0, ROWS - PIECE)], recv_sem.at[2]
        ).wait()

    @pl.when(me > 1)
    def _():
        pltpu.make_async_remote_copy(
            anchor.at[core], anchor.at[core], send_sem.at[4], recv_sem.at[3],
            device_id=at_hst(me + 1 - 2 * core), device_id_type=MESH,
        ).start()

    pltpu.make_async_copy(
        got_b.at[pl.ds(0, HST - 1)], got_b.at[pl.ds(0, HST - 1)], recv_sem.at[4]
    ).wait()
    terms = got_b[...].astype(jnp.float32)
    value, stat = terms[:, :8], terms[:, 8:]
    turned = pltpu.roll(stat, HD // 2, 2)
    low = lax.broadcasted_iota(jnp.int32, stat.shape, 2) < HD // 2
    peaks = jnp.where(low, stat, turned)
    sums = jnp.where(low, turned, stat)
    factor = jnp.exp2(peaks - jnp.max(peaks, axis=0, keepdims=True))
    attended = jnp.sum(factor * value, axis=0) / jnp.sum(factor * sums, axis=0)
    att[pl.ds(me, 1)] = attended.astype(jnp.bfloat16)[None]

    @pl.loop(1, HST)
    def _(k):
        pltpu.make_async_remote_copy(
            att.at[me], att.at[me], send_sem.at[6], recv_sem.at[5],
            device_id=at_hst(lax.rem(me + k, HST)), device_id_type=MESH,
        ).start()

    @pl.when(me > 0)
    def _():
        pltpu.make_async_copy(anchor.at[0], anchor.at[0], recv_sem.at[3]).wait()

    finish_head(0)

    load_w.wait()
    pltpu.make_async_copy(
        att.at[pl.ds(0, HST - 1)], att.at[pl.ds(0, HST - 1)], recv_sem.at[5]
    ).wait()
    rows = att[...].astype(jnp.float32).reshape(HEADS, QN, HD)
    wide = jnp.concatenate([rows[h] for h in range(HEADS)], axis=1).astype(jnp.bfloat16)
    partial = dot(wide, weight[...])
    for t in range(TP):
        r, c = t // 2, t % 2
        part[t] = partial[r * 8 : r * 8 + 8, c * HD : (c + 1) * HD].astype(jnp.bfloat16)

    @pl.loop(1, TP)
    def _(k):
        d = lax.rem(z + k, TP)
        pltpu.make_async_remote_copy(
            part.at[d], got_d.at[z], send_sem.at[7], recv_sem.at[6],
            device_id=at_tp(d), device_id_type=MESH,
        ).start()

    got_d[pl.ds(z, 1)] = part[pl.ds(z, 1)]
    finish_head(1)

    pltpu.make_async_copy(
        got_d.at[pl.ds(0, TP - 1)], got_d.at[pl.ds(0, TP - 1)], recv_sem.at[6]
    ).wait()
    total = jnp.sum(got_d[...].astype(jnp.float32), axis=0)
    got_e[pl.ds(z, 1)] = total.astype(jnp.bfloat16)[None]

    @pl.loop(1, TP)
    def _(k):
        pltpu.make_async_remote_copy(
            got_e.at[z], got_e.at[z], send_sem.at[8], recv_sem.at[7],
            device_id=at_tp(lax.rem(z + k, TP)), device_id_type=MESH,
        ).start()

    finish_head(2)
    finish_head(3)

    pltpu.make_async_copy(
        got_e.at[pl.ds(0, TP - 1)], got_e.at[pl.ds(0, TP - 1)], recv_sem.at[7]
    ).wait()
    tiles = got_e[...].astype(jnp.float32)
    qout[...] = jnp.concatenate(
        [
            jnp.concatenate([tiles[2 * r], tiles[2 * r + 1]], axis=1)
            for r in range(TP // 2)
        ],
        axis=0,
    ).astype(jnp.bfloat16)
    save_q = pltpu.make_async_copy(qout, query_out, local_sem.at[5])
    save_q.start()

    for sem, ref in (
        (0, gather_q.at[pl.ds(0, HST - 1)]),
        (5, got_b.at[pl.ds(0, HST - 1)]),
        (6, att.at[pl.ds(0, HST - 1)]),
        (7, got_d.at[pl.ds(0, TP - 1)]),
        (8, got_e.at[pl.ds(0, TP - 1)]),
    ):
        pltpu.make_async_copy(ref, ref, send_sem.at[sem]).wait()

    def sent(sem, rows):
        ref = own.at[0, pl.ds(0, rows)]
        pltpu.make_async_copy(ref, ref, send_sem.at[sem]).wait()

    @pl.when(me == 0)
    def _():
        sent(1, ROWS - PIECE)
        sent(2, ROWS)

    @pl.when(core + (me == 0) > 0)
    def _():
        sent(3, ROWS - PIECE)

    @pl.when(core + (me == 0) == 0)
    def _():
        sent(3, ROWS - 2 * PIECE)

    @pl.when((me == 0) | (me > 1))
    def _():
        sent(4, ROWS)

    save_q.wait()
    for h in range(HEADS):
        pltpu.make_async_copy(
            enc.at[:, pl.ds(h * HD, HD)], ctx_out.at[:, pl.ds(h * HD, HD)], out_sem.at[h]
        ).wait()


def per_device(ctx_q, ctx_kv, lengths, query_q, query_kv, out_weight):
    bf16, f32 = jnp.bfloat16, jnp.float32
    any_space = pl.BlockSpec(memory_space=pl.ANY)
    return pl.pallas_call(
        kernel,
        out_shape=(
            jax.ShapeDtypeStruct((ROWS, HEADS * HD), bf16),
            jax.ShapeDtypeStruct((QN, COLS), bf16),
        ),
        in_specs=[pl.BlockSpec(memory_space=pltpu.SMEM)] + [any_space] * 5,
        out_specs=(any_space, any_space),
        scratch_shapes=[
            pltpu.VMEM((ROWS, HEADS * HD), bf16),
            pltpu.VMEM((2, ROWS, HD), bf16),
            pltpu.VMEM((2, ROWS, HD), bf16),
            pltpu.VMEM((HEADS * HD, COLS), bf16),
            pltpu.VMEM((2, HEADS * HD), bf16),
            pltpu.VMEM((2, 2, KVH * HD), bf16),
            pltpu.VMEM((2, HD, HD), bf16),
            pltpu.VMEM((HEADS, ROWS, HD), f32),
            pltpu.VMEM((HEADS, ROWS, HD), f32),
            pltpu.VMEM((HEADS, ROWS, HD), f32),
            pltpu.VMEM((ROWS, HEADS * HD), bf16),
            pltpu.VMEM((HST, 8, HD), bf16),
            pltpu.VMEM((HST * 8, HD), f32),
            pltpu.VMEM((HST, 16, HD), bf16),
            pltpu.VMEM((HST, 16, HD), bf16),
            pltpu.VMEM((HST, 8, HD), bf16),
            pltpu.VMEM((TP, 8, HD), bf16),
            pltpu.VMEM((TP, 8, HD), bf16),
            pltpu.VMEM((TP, 8, HD), bf16),
            pltpu.VMEM((QN, COLS), bf16),
            pltpu.SemaphoreType.DMA((6,)),
            pltpu.SemaphoreType.DMA((HEADS,)),
            pltpu.SemaphoreType.DMA((9,)),
            pltpu.SemaphoreType.DMA((8,)),
        ],
        compiler_params=pltpu.CompilerParams(
            collective_id=0, has_side_effects=True, vmem_limit_bytes=40 * 1024 * 1024
        ),
    )(lengths, ctx_q, ctx_kv, query_q, query_kv, out_weight)


def solution(mesh):
    return jax.shard_map(
        per_device,
        mesh=mesh,
        in_specs=(
            P("hst", "tp"),
            P(None, "hst", None),
            P(),
            P("hst", "tp"),
            P(None, "hst", None),
            P("tp", "hst"),
        ),
        out_specs=(P("hst", "tp"), P(None, "hst")),
        check_vma=False,
    )
```

time: 399 us -> 57.2 us (0.14)
  blocking collectives: 201 us -> 0 us
  waiting for transfers between devices: 154 us -> 0 us
  Pallas kernels: 0 us -> 48.3 us
  matrix products: 14.7 us -> 0 us
  between operations: 14.2 us -> 0.65 us
  other arithmetic: 11.8 us -> 0 us
  local copies, waits for them, and re-layouts: 2.66 us -> 7.49 us
    psum x2 -> x0, waiting for transfers between devices: 154 us -> none  [the longest x1 91.2 us: spread(): return lax.psum(kept, axis)]
    psum x2 -> x0, blocking collectives: 110 us -> none  [the longest x1 65.3 us: per_device(): lax.psum((totals * factor, outputs * factor[..., None]), 'hst')]
    pmax x1 -> x0, blocking collectives: 62.2 us -> none  [per_device(): highest = lax.pmax(maxima, 'hst')]
    pallas_call x0 -> x1, Pallas kernels: none -> 48.3 us  [per_device(): pl.pallas_call(kernel, out_shape=(jax.ShapeDtypeStruct((ROWS, HEADS * HD)...]
    all_gather x1 -> x0, blocking collectives: 28.5 us -> none  [per_device(): all_queries = lax.all_gather(query_q, 'hst', axis=0, tiled=True)]
    dot_general x17 -> x0, matrix products: 14.7 us -> none  [the longest x4 6.66 us: encode_head(): jnp.einsum('ij,jd->id', probs, joined[1, kv_index], preferred_element_typ...]
    unnamed x5 -> x14, local copies, waits for them, and re-layouts: 0.29 us -> 7.49 us
    select_n x2 -> x0, other arithmetic: 4.12 us -> none  [the longest x1 2.26 us: per_device(): jnp.where((row_ids < own_len)[:, None], encoded, jnp.zeros_like(encoded))]
  transfers between devices with their start and end apart: 2 -> 0, of which waited for: 2 -> 0; matrix products, arithmetic and copies ran while one was open for 1% -> 0% of each run, Pallas kernels for 0% -> 0%
where the time goes in v1:
time: 57.2 us; the launch traced here: 56.5 us
  Pallas kernels  48.3 us (84%)
  local copies, waits for them, and re-layouts  7.49 us (13%)
  between operations  0.65 us (1%)
    pallas_call x1, Pallas kernels, per_device(): pl.pallas_call(kernel, out_shape=(jax.ShapeDtypeStruct((ROWS, HEADS * HD)...  48.3 us
    unnamed x14, local copies, waits for them, and re-layouts  7.49 us

profile of v1, /device:TPU:1, one launch (start us, length us, event | category | flops | bytes accessed | tf_op | source)
XLA Modules:
  0.0 56.5 jit_solution(13307056810623080720)
XLA Ops:
  0.6 0.0 copy-start
  0.6 1.9 %copy-done = bf16[2,768,1024]{2,1,0:T(8,128)(2,1)S(1)} copy-done((bf16[2,768,1024]{2,1,0:T(8,128)(2,1)S(1)}, bf16[2,768,1024]{2,1,0:T(8,128)(2,1)}, u32[]{:S(2)}) %copy-start) | copy-done | bytes 3145752
  2.5 0.0 copy-start.1
  2.5 1.1 %copy-done.1 = bf16[768,512]{1,0:T(8,128)(2,1)S(1)} copy-done((bf16[768,512]{1,0:T(8,128)(2,1)S(1)}, bf16[768,512]{1,0:T(8,128)(2,1)}, u32[]{:S(2)}) %copy-start.1) | copy-done | bytes 786456
  3.7 0.0 copy-start.2
  3.7 0.9 %copy-done.2 = bf16[512,256]{1,0:T(8,128)(2,1)S(1)} copy-done((bf16[512,256]{1,0:T(8,128)(2,1)S(1)}, bf16[512,256]{1,0:T(8,128)(2,1)}, u32[]{:S(2)}) %copy-start.2) | copy-done | bytes 262168
  4.6 0.0 copy-start.3
  4.6 0.7 %copy-done.3 = bf16[2,2,1024]{2,1,0:T(2,128)(2,1)S(1)} copy-done((bf16[2,2,1024]{2,1,0:T(2,128)(2,1)S(1)}, bf16[2,2,1024]{2,1,0:T(2,128)(2,1)}, u32[]{:S(2)}) %copy-start.3) | copy-done | bytes 8216
  5.3 0.0 copy-start.4
  5.3 0.7 %copy-done.4 = bf16[2,512]{1,0:T(2,128)(2,1)S(1)} copy-done((bf16[2,512]{1,0:T(2,128)(2,1)S(1)}, bf16[2,512]{1,0:T(2,128)(2,1)}, u32[]{:S(2)}) %copy-start.4) | copy-done | bytes 2072
  6.0 0.0 copy-start.5
  6.0 0.7 %copy-done.5 = s32[32]{0:T(128)S(1)} copy-done((s32[32]{0:T(128)S(1)}, s32[32]{0:T(128)}, u32[]{:S(2)}) %copy-start.5) | copy-done | bytes 152
  6.6 48.3 %shard_map.77 = (bf16[768,512]{1,0:T(8,128)(2,1)S(1)}, bf16[64,256]{1,0:T(8,128)(2,1)S(1)}) custom-call(s32[32]{0:T(128)S(1)} %copy-done.5, bf16[768,512]{1,0:T(8,128)(2,1)S(1)} %copy-done.1, bf16[2,768,1024]{2,1,0:T(8,128)(2,1)S(1)} %copy-done, bf16[2,512]{1,0:T(2,128)(2,1)S(1)} %copy-done.4, bf16[2,2,1024]{2,1,0:T(2,128)(2,1)S(1)} %copy-done.3, ...), custom_call_target="tpu_custom_call" | custom-call | tf_op jit(solution)/shard_map/pallas_call | solution.py:411
  55.0 0.9 %copy.10 = bf16[768,512]{1,0:T(8,128)(2,1)} copy(bf16[768,512]{1,0:T(8,128)(2,1)S(1)} %get-tuple-element.4) | data formatting | bytes 1572864
  55.9 0.6 %copy.11 = bf16[64,256]{1,0:T(8,128)(2,1)} copy(bf16[64,256]{1,0:T(8,128)(2,1)S(1)} %get-tuple-element.5) | data formatting | bytes 65536
Async XLA Ops:
  0.6 1.9 %copy-start = (bf16[2,768,1024]{2,1,0:T(8,128)(2,1)S(1)}, bf16[2,768,1024]{2,1,0:T(8,128)(2,1)}, u32[]{:S(2)}) copy-start(bf16[2,768,1024]{2,1,0:T(8,128)(2,1)} %ctx_kv.1) | copy-start | bytes 9437188
  2.5 1.1 %copy-start.1 = (bf16[768,512]{1,0:T(8,128)(2,1)S(1)}, bf16[768,512]{1,0:T(8,128)(2,1)}, u32[]{:S(2)}) copy-start(bf16[768,512]{1,0:T(8,128)(2,1)} %ctx_q.1) | copy-start | bytes 2359300
  3.7 0.9 %copy-start.2 = (bf16[512,256]{1,0:T(8,128)(2,1)S(1)}, bf16[512,256]{1,0:T(8,128)(2,1)}, u32[]{:S(2)}) copy-start(bf16[512,256]{1,0:T(8,128)(2,1)} %out_weight.1) | copy-start | bytes 786436
  4.6 0.7 %copy-start.3 = (bf16[2,2,1024]{2,1,0:T(2,128)(2,1)S(1)}, bf16[2,2,1024]{2,1,0:T(2,128)(2,1)}, u32[]{:S(2)}) copy-start(bf16[2,2,1024]{2,1,0:T(2,128)(2,1)} %query_kv.1) | copy-start | bytes 24580
  5.3 0.7 %copy-start.4 = (bf16[2,512]{1,0:T(2,128)(2,1)S(1)}, bf16[2,512]{1,0:T(2,128)(2,1)}, u32[]{:S(2)}) copy-start(bf16[2,512]{1,0:T(2,128)(2,1)} %query_q.1) | copy-start | bytes 6148
  6.0 0.7 %copy-start.5 = (s32[32]{0:T(128)S(1)}, s32[32]{0:T(128)}, u32[]{:S(2)}) copy-start(s32[32]{0:T(128)} %lengths.1) | copy-start | bytes 388

commit v2 on v1

--- a/solution.py
+++ b/solution.py
@@ -22,6 +22,13 @@
 MESH = pl.DeviceIdType.MESH
 
 
+PLANE = sorted(
+    [(y, x, c) for y in range(4) for x in range(4) for c in range(2) if y or x or c],
+    key=lambda o: -(min(o[0], 4 - o[0]) + min(o[1], 4 - o[1]) + 0.1 * o[2]),
+)
+ALONG = sorted(range(1, TP), key=lambda o: -min(o, TP - o))
+
+
 def dot_t(a, b):
     return lax.dot_general(a, b, (((1,), (1,)), ((), ())), preferred_element_type=jnp.float32)
 
@@ -35,7 +42,7 @@
 
 
 def kernel(
-    lengths,
+    lengths_hbm,
     ctx_q,
     ctx_kv,
     query_q,
@@ -43,6 +50,7 @@
     out_weight,
     ctx_out,
     query_out,
+    lengths,
     cq,
     own,
     anchor,
@@ -53,7 +61,6 @@
     out1,
     sum1,
     max1,
-    enc,
     gather_q,
     rows_q,
     sent_b,
@@ -62,9 +69,7 @@
     part,
     got_d,
     got_e,
-    qout,
     local_sem,
-    out_sem,
     send_sem,
     recv_sem,
 ):
@@ -74,6 +79,16 @@
     core = lax.rem(me, 2)
     kv_off = pl.multiple_of((z // 2) * HD, HD)
 
+    py, px = chip // 4, lax.rem(chip, 4)
+
+    def plane_peers():
+        for dy, dx, dc in PLANE:
+            yield lax.rem(py + dy, 4) * 8 + lax.rem(px + dx, 4) * 2 + lax.rem(core + dc, 2)
+
+    def along_peers():
+        for dz in ALONG:
+            yield lax.rem(z + dz, TP)
+
     def at_hst(d):
         return {"hst": d}
 
@@ -85,23 +100,18 @@
     load_qq = pltpu.make_async_copy(query_q, qq, local_sem.at[2])
     load_qkv = pltpu.make_async_copy(query_kv, qkv, local_sem.at[3])
     load_w = pltpu.make_async_copy(out_weight, weight, local_sem.at[4])
-    for copy in (load_qq, load_kv, load_cq, load_qkv, load_w):
+    load_len = pltpu.make_async_copy(lengths_hbm, lengths, local_sem.at[6])
+    for copy in (load_len, load_qq, load_kv, load_cq, load_qkv, load_w):
         copy.start()
 
     barrier = pltpu.get_barrier_semaphore()
 
-    @pl.loop(1, HST)
-    def _(k):
-        pl.semaphore_signal(
-            barrier, inc=1, device_id=at_hst(lax.rem(me + k, HST)), device_id_type=MESH
-        )
-
-    @pl.loop(1, TP)
-    def _(k):
-        pl.semaphore_signal(
-            barrier, inc=1, device_id=at_tp(lax.rem(z + k, TP)), device_id_type=MESH
-        )
-
+    for d in plane_peers():
+        pl.semaphore_signal(barrier, inc=1, device_id=at_hst(d), device_id_type=MESH)
+    for d in along_peers():
+        pl.semaphore_signal(barrier, inc=1, device_id=at_tp(d), device_id_type=MESH)
+
+    load_len.wait()
     own_len = lengths[me]
 
     diag_row = lax.broadcasted_iota(jnp.int32, (TILE, TILE), 0)
@@ -138,12 +148,12 @@
             keep = jnp.exp2(before - m)
             num = out1[h, rows, :] * keep + o[:, :HD]
             den = sum1[h, rows, :] * keep + o[:, HD:]
-            enc[rows, h * HD : (h + 1) * HD] = live(rb, num / den)
+            ctx_out[rows, h * HD : (h + 1) * HD] = live(rb, num / den)
 
     def first_head(h):
         for rb in range(ROWS // TILE):
             rows = pl.ds(rb * TILE, TILE)
-            enc[rows, h * HD : (h + 1) * HD] = live(rb, out1[h, rows, :] / sum1[h, rows, :])
+            ctx_out[rows, h * HD : (h + 1) * HD] = live(rb, out1[h, rows, :] / sum1[h, rows, :])
 
     def finish_head(h):
         @pl.when(me > 0)
@@ -153,10 +163,6 @@
         @pl.when(me == 0)
         def _():
             first_head(h)
-
-        pltpu.make_async_copy(
-            enc.at[:, pl.ds(h * HD, HD)], ctx_out.at[:, pl.ds(h * HD, HD)], out_sem.at[h]
-        ).start()
 
     load_qq.wait()
     mine = qq[...].astype(jnp.float32)
@@ -164,21 +170,18 @@
         [mine[t : t + 1, h * HD : (h + 1) * HD] for t in range(2) for h in range(HEADS)], axis=0
     ).astype(jnp.bfloat16)[None]
 
-    load_kv.wait()
-    load_cq.wait()
-    own_head(0)
-
     pl.semaphore_wait(barrier, HST - 1 + TP - 1)
 
-    @pl.loop(1, HST)
-    def _(k):
+    for d in plane_peers():
         pltpu.make_async_remote_copy(
             gather_q.at[me], gather_q.at[me], send_sem.at[0], recv_sem.at[0],
-            device_id=at_hst(lax.rem(me + k, HST)), device_id_type=MESH,
+            device_id=at_hst(d), device_id_type=MESH,
         ).start()
 
     def piece(ref, plane, c):
         return ref.at[plane, pl.ds(pl.multiple_of(c * PIECE, 16), PIECE), :]
+
+    load_kv.wait()
 
     @pl.when(me == 0)
     def _():
@@ -210,26 +213,9 @@
             device_id=at_hst(1), device_id_type=MESH,
         ).start()
 
-    own_head(1)
-    own_head(2)
-
-    @pl.when(me > 0)
-    def _():
-        pltpu.make_async_copy(
-            piece(anchor, 0, 0), piece(anchor, 0, 0), recv_sem.at[1]
-        ).wait()
-
-        @pl.loop(1, CHIPS)
-        def _(k):
-            c = lax.rem(chip + k, CHIPS)
-
-            @pl.when(c * 2 + core > 0)
-            def _():
-                pltpu.make_async_remote_copy(
-                    piece(anchor, core, chip), piece(anchor, core, chip),
-                    send_sem.at[3], recv_sem.at[2],
-                    device_id=at_hst(c * 2 + core), device_id_type=MESH,
-                ).start()
+    load_cq.wait()
+    for h in range(HEADS):
+        own_head(h)
 
     pltpu.make_async_copy(
         gather_q.at[pl.ds(0, HST - 1)], gather_q.at[pl.ds(0, HST - 1)], recv_sem.at[0]
@@ -265,9 +251,7 @@
         [o[:, :HD].reshape(HST, 8, HD), stats.reshape(HST, 8, HD)], axis=1
     ).astype(jnp.bfloat16)
 
-    @pl.loop(1, HST)
-    def _(k):
-        d = lax.rem(me + k, HST)
+    for d in plane_peers():
         pltpu.make_async_remote_copy(
             sent_b.at[d], got_b.at[me], send_sem.at[5], recv_sem.at[4],
             device_id=at_hst(d), device_id_type=MESH,
@@ -275,20 +259,23 @@
 
     got_b[pl.ds(me, 1)] = sent_b[pl.ds(me, 1)]
 
-    own_head(3)
-
     @pl.when(me > 0)
     def _():
         pltpu.make_async_copy(
-            anchor.at[0, pl.ds(0, ROWS - PIECE)], anchor.at[0, pl.ds(0, ROWS - PIECE)], recv_sem.at[2]
+            piece(anchor, 0, 0), piece(anchor, 0, 0), recv_sem.at[1]
         ).wait()
 
-    @pl.when(me > 1)
-    def _():
-        pltpu.make_async_remote_copy(
-            anchor.at[core], anchor.at[core], send_sem.at[4], recv_sem.at[3],
-            device_id=at_hst(me + 1 - 2 * core), device_id_type=MESH,
-        ).start()
+        @pl.loop(1, CHIPS)
+        def _(k):
+            c = lax.rem(chip + k, CHIPS)
+
+            @pl.when(c * 2 + core > 0)
+            def _():
+                pltpu.make_async_remote_copy(
+                    piece(anchor, core, chip), piece(anchor, core, chip),
+                    send_sem.at[3], recv_sem.at[2],
+                    device_id=at_hst(c * 2 + core), device_id_type=MESH,
+                ).start()
 
     pltpu.make_async_copy(
         got_b.at[pl.ds(0, HST - 1)], got_b.at[pl.ds(0, HST - 1)], recv_sem.at[4]
@@ -303,18 +290,24 @@
     attended = jnp.sum(factor * value, axis=0) / jnp.sum(factor * sums, axis=0)
     att[pl.ds(me, 1)] = attended.astype(jnp.bfloat16)[None]
 
-    @pl.loop(1, HST)
-    def _(k):
+    for d in plane_peers():
         pltpu.make_async_remote_copy(
             att.at[me], att.at[me], send_sem.at[6], recv_sem.at[5],
-            device_id=at_hst(lax.rem(me + k, HST)), device_id_type=MESH,
+            device_id=at_hst(d), device_id_type=MESH,
         ).start()
 
     @pl.when(me > 0)
     def _():
-        pltpu.make_async_copy(anchor.at[0], anchor.at[0], recv_sem.at[3]).wait()
-
-    finish_head(0)
+        pltpu.make_async_copy(
+            anchor.at[0, pl.ds(0, ROWS - PIECE)], anchor.at[0, pl.ds(0, ROWS - PIECE)], recv_sem.at[2]
+        ).wait()
+
+    @pl.when(me > 1)
+    def _():
+        pltpu.make_async_remote_copy(
+            anchor.at[core], anchor.at[core], send_sem.at[4], recv_sem.at[3],
+            device_id=at_hst(me + 1 - 2 * core), device_id_type=MESH,
+        ).start()
 
     load_w.wait()
     pltpu.make_async_copy(
@@ -327,15 +320,18 @@
         r, c = t // 2, t % 2
         part[t] = partial[r * 8 : r * 8 + 8, c * HD : (c + 1) * HD].astype(jnp.bfloat16)
 
-    @pl.loop(1, TP)
-    def _(k):
-        d = lax.rem(z + k, TP)
+    for d in along_peers():
         pltpu.make_async_remote_copy(
             part.at[d], got_d.at[z], send_sem.at[7], recv_sem.at[6],
             device_id=at_tp(d), device_id_type=MESH,
         ).start()
 
     got_d[pl.ds(z, 1)] = part[pl.ds(z, 1)]
+    @pl.when(me > 0)
+    def _():
+        pltpu.make_async_copy(anchor.at[0], anchor.at[0], recv_sem.at[3]).wait()
+
+    finish_head(0)
     finish_head(1)
 
     pltpu.make_async_copy(
@@ -344,11 +340,10 @@
     total = jnp.sum(got_d[...].astype(jnp.float32), axis=0)
     got_e[pl.ds(z, 1)] = total.astype(jnp.bfloat16)[None]
 
-    @pl.loop(1, TP)
-    def _(k):
+    for d in along_peers():
         pltpu.make_async_remote_copy(
             got_e.at[z], got_e.at[z], send_sem.at[8], recv_sem.at[7],
-            device_id=at_tp(lax.rem(z + k, TP)), device_id_type=MESH,
+            device_id=at_tp(d), device_id_type=MESH,
         ).start()
 
     finish_head(2)
@@ -358,15 +353,13 @@
         got_e.at[pl.ds(0, TP - 1)], got_e.at[pl.ds(0, TP - 1)], recv_sem.at[7]
     ).wait()
     tiles = got_e[...].astype(jnp.float32)
-    qout[...] = jnp.concatenate(
+    query_out[...] = jnp.concatenate(
         [
             jnp.concatenate([tiles[2 * r], tiles[2 * r + 1]], axis=1)
             for r in range(TP // 2)
         ],
         axis=0,
     ).astype(jnp.bfloat16)
-    save_q = pltpu.make_async_copy(qout, query_out, local_sem.at[5])
-    save_q.start()
 
     for sem, ref in (
         (0, gather_q.at[pl.ds(0, HST - 1)]),
@@ -398,25 +391,21 @@
     def _():
         sent(4, ROWS)
 
-    save_q.wait()
-    for h in range(HEADS):
-        pltpu.make_async_copy(
-            enc.at[:, pl.ds(h * HD, HD)], ctx_out.at[:, pl.ds(h * HD, HD)], out_sem.at[h]
-        ).wait()
-
 
 def per_device(ctx_q, ctx_kv, lengths, query_q, query_kv, out_weight):
     bf16, f32 = jnp.bfloat16, jnp.float32
-    any_space = pl.BlockSpec(memory_space=pl.ANY)
+    hbm = pl.BlockSpec(memory_space=pltpu.HBM)
+    vmem = pl.BlockSpec(memory_space=pltpu.VMEM)
     return pl.pallas_call(
         kernel,
         out_shape=(
-            jax.ShapeDtypeStruct((ROWS, HEADS * HD), bf16),
-            jax.ShapeDtypeStruct((QN, COLS), bf16),
+            pltpu.VMEM((ROWS, HEADS * HD), bf16),
+            pltpu.VMEM((QN, COLS), bf16),
         ),
-        in_specs=[pl.BlockSpec(memory_space=pltpu.SMEM)] + [any_space] * 5,
-        out_specs=(any_space, any_space),
+        in_specs=[hbm] * 6,
+        out_specs=(vmem, vmem),
         scratch_shapes=[
+            pltpu.SMEM((HST,), jnp.int32),
             pltpu.VMEM((ROWS, HEADS * HD), bf16),
             pltpu.VMEM((2, ROWS, HD), bf16),
             pltpu.VMEM((2, ROWS, HD), bf16),
@@ -427,7 +416,6 @@
             pltpu.VMEM((HEADS, ROWS, HD), f32),
             pltpu.VMEM((HEADS, ROWS, HD), f32),
             pltpu.VMEM((HEADS, ROWS, HD), f32),
-            pltpu.VMEM((ROWS, HEADS * HD), bf16),
             pltpu.VMEM((HST, 8, HD), bf16),
             pltpu.VMEM((HST * 8, HD), f32),
             pltpu.VMEM((HST, 16, HD), bf16),
@@ -436,16 +424,14 @@
             pltpu.VMEM((TP, 8, HD), bf16),
             pltpu.VMEM((TP, 8, HD), bf16),
             pltpu.VMEM((TP, 8, HD), bf16),
-            pltpu.VMEM((QN, COLS), bf16),
-            pltpu.SemaphoreType.DMA((6,)),
-            pltpu.SemaphoreType.DMA((HEADS,)),
+            pltpu.SemaphoreType.DMA((7,)),
             pltpu.SemaphoreType.DMA((9,)),
             pltpu.SemaphoreType.DMA((8,)),
         ],
         compiler_params=pltpu.CompilerParams(
-            collective_id=0, has_side_effects=True, vmem_limit_bytes=40 * 1024 * 1024
+            collective_id=0, has_side_effects=True, vmem_limit_bytes=48 * 1024 * 1024
         ),
-    )(lengths, ctx_q, ctx_kv, query_q, query_kv, out_weight)
+    )(*(pltpu.with_memory_space_constraint(a, pltpu.HBM) for a in (lengths, ctx_q, ctx_kv, query_q, query_kv, out_weight)))
 
 
 def solution(mesh):

time: 57.2 us -> 48.8 us (0.85)
  local copies, waits for them, and re-layouts: 7.49 us -> 1.5 us
  Pallas kernels: 48.3 us -> 46.3 us
    unnamed x14 -> x2, local copies, waits for them, and re-layouts: 7.49 us -> 1.5 us
    pallas_call x1, Pallas kernels: 48.3 us -> 46.3 us  [per_device(): pl.pallas_call(kernel, out_shape=(pltpu.VMEM((ROWS, HEADS * HD), bf16), p...]
where the time goes in v2:
time: 48.8 us; the launch traced here: 48.4 us
  Pallas kernels  46.3 us (95%)
  local copies, waits for them, and re-layouts  1.5 us (3%)
  between operations  0.64 us (1%)
    pallas_call x1, Pallas kernels, per_device(): pl.pallas_call(kernel, out_shape=(pltpu.VMEM((ROWS, HEADS * HD), bf16), p...  46.3 us
    unnamed x2, local copies, waits for them, and re-layouts  1.5 us

profile of v2, /device:TPU:1, one launch (start us, length us, event | category | flops | bytes accessed | tf_op | source)
XLA Modules:
  0.0 48.4 jit_solution(16828544552032158738)
XLA Ops:
  0.6 46.3 %shard_map.77 = (bf16[768,512]{1,0:T(8,128)(2,1)S(1)}, bf16[64,256]{1,0:T(8,128)(2,1)S(1)}) custom-call(s32[32]{0:T(128)} %lengths_hbm.1, bf16[768,512]{1,0:T(8,128)(2,1)} %ctx_q.1, bf16[2,768,1024]{2,1,0:T(8,128)(2,1)} %ctx_kv.1, bf16[2,512]{1,0:T(2,128)(2,1)} %query_q.1, bf16[2,2,1024]{2,1,0:T(2,128)(2,1)} %query_kv.1, bf16[512,256]{1,0:T(8,128)(2,1)} %out_weight.1), custom_call_target="tpu_custom_call" | custom-call | tf_op jit(solution)/shard_map/pallas_call | solution.py:399
  46.9 0.9 %copy.10 = bf16[768,512]{1,0:T(8,128)(2,1)} copy(bf16[768,512]{1,0:T(8,128)(2,1)S(1)} %get-tuple-element.2) | data formatting | bytes 1572864
  47.8 0.6 %copy.11 = bf16[64,256]{1,0:T(8,128)(2,1)} copy(bf16[64,256]{1,0:T(8,128)(2,1)S(1)} %get-tuple-element.3) | data formatting | bytes 65536

commit v3 on v2

--- a/solution.py
+++ b/solution.py
@@ -22,11 +22,12 @@
 MESH = pl.DeviceIdType.MESH
 
 
-PLANE = sorted(
-    [(y, x, c) for y in range(4) for x in range(4) for c in range(2) if y or x or c],
-    key=lambda o: -(min(o[0], 4 - o[0]) + min(o[1], 4 - o[1]) + 0.1 * o[2]),
+CHIP_OFFSETS = sorted(
+    [(y, x) for y in range(4) for x in range(4) if y or x],
+    key=lambda o: -(min(o[0], 4 - o[0]) + min(o[1], 4 - o[1])),
 )
-ALONG = sorted(range(1, TP), key=lambda o: -min(o, TP - o))
+TILES = 8
+FIRST = 11
 
 
 def dot_t(a, b):
@@ -68,10 +69,12 @@
     att,
     part,
     got_d,
+    summed,
     got_e,
     local_sem,
     send_sem,
     recv_sem,
+    ready,
 ):
     me = lax.axis_index("hst")
     z = lax.axis_index("tp")
@@ -81,19 +84,17 @@
 
     py, px = chip // 4, lax.rem(chip, 4)
 
-    def plane_peers():
-        for dy, dx, dc in PLANE:
-            yield lax.rem(py + dy, 4) * 8 + lax.rem(px + dx, 4) * 2 + lax.rem(core + dc, 2)
-
-    def along_peers():
-        for dz in ALONG:
-            yield lax.rem(z + dz, TP)
+    mate = me + 1 - 2 * core
+    column = chip * 2 + 1
+    tile = lax.rem(z + TP - FIRST, TP)
+    adds = (core == 1) & (tile < TILES)
+
+    def other_chips():
+        for dy, dx in CHIP_OFFSETS:
+            yield lax.rem(py + dy, 4) * 4 + lax.rem(px + dx, 4)
 
     def at_hst(d):
         return {"hst": d}
-
-    def at_tp(d):
-        return {"tp": d}
 
     load_kv = pltpu.make_async_copy(ctx_kv.at[:, :, pl.ds(kv_off, HD)], own, local_sem.at[0])
     load_cq = pltpu.make_async_copy(ctx_q, cq, local_sem.at[1])
@@ -106,10 +107,14 @@
 
     barrier = pltpu.get_barrier_semaphore()
 
-    for d in plane_peers():
-        pl.semaphore_signal(barrier, inc=1, device_id=at_hst(d), device_id_type=MESH)
-    for d in along_peers():
-        pl.semaphore_signal(barrier, inc=1, device_id=at_tp(d), device_id_type=MESH)
+    def greet(**where):
+        pl.semaphore_signal(barrier, inc=1, device_id=where, device_id_type=MESH)
+
+    for c in other_chips():
+        greet(hst=c * 2)
+    for dz in (8, 7, 9, 6, 10, 5, 11, 4, 12, 3, 13, 2, 14, 1, 15):
+        greet(hst=column, tp=lax.rem(z + dz, TP))
+    greet(hst=mate)
 
     load_len.wait()
     own_len = lengths[me]
@@ -170,13 +175,25 @@
         [mine[t : t + 1, h * HD : (h + 1) * HD] for t in range(2) for h in range(HEADS)], axis=0
     ).astype(jnp.bfloat16)[None]
 
-    pl.semaphore_wait(barrier, HST - 1 + TP - 1)
-
-    for d in plane_peers():
+    @pl.when(core == 0)
+    def _():
+        pl.semaphore_wait(barrier, HST - 1)
+        pl.semaphore_signal(ready.at[0], inc=1, device_id=at_hst(mate), device_id_type=MESH)
+
+    @pl.when(core == 1)
+    def _():
+        pl.semaphore_wait(ready.at[0], 1)
+
+    def send_a(d):
         pltpu.make_async_remote_copy(
             gather_q.at[me], gather_q.at[me], send_sem.at[0], recv_sem.at[0],
             device_id=at_hst(d), device_id_type=MESH,
         ).start()
+
+    for c in other_chips():
+        send_a(c * 2)
+        send_a(c * 2 + 1)
+    send_a(mate)
 
     def piece(ref, plane, c):
         return ref.at[plane, pl.ds(pl.multiple_of(c * PIECE, 16), PIECE), :]
@@ -248,16 +265,25 @@
     lane = lax.broadcasted_iota(jnp.int32, (HEADS * QN, HD), 1)
     stats = jnp.where(lane < HD // 2, jnp.broadcast_to(peak, (HEADS * QN, HD)), o[:, HD:])
     sent_b[...] = jnp.concatenate(
-        [o[:, :HD].reshape(HST, 8, HD), stats.reshape(HST, 8, HD)], axis=1
+        [o[:, :HD].reshape(CHIPS, 16, HD), stats.reshape(CHIPS, 16, HD)], axis=1
     ).astype(jnp.bfloat16)
 
-    for d in plane_peers():
-        pltpu.make_async_remote_copy(
-            sent_b.at[d], got_b.at[me], send_sem.at[5], recv_sem.at[4],
-            device_id=at_hst(d), device_id_type=MESH,
-        ).start()
-
-    got_b[pl.ds(me, 1)] = sent_b[pl.ds(me, 1)]
+    def send_b(c):
+        pltpu.make_async_remote_copy(
+            sent_b.at[c], got_b.at[me], send_sem.at[5], recv_sem.at[4],
+            device_id=at_hst(c * 2 + 1), device_id_type=MESH,
+        ).start()
+
+    for c in other_chips():
+        send_b(c)
+
+    @pl.when(core == 0)
+    def _():
+        send_b(chip)
+
+    @pl.when(core == 1)
+    def _():
+        got_b[pl.ds(me, 1)] = sent_b[pl.ds(chip, 1)]
 
     @pl.when(me > 0)
     def _():
@@ -277,24 +303,31 @@
                     device_id=at_hst(c * 2 + core), device_id_type=MESH,
                 ).start()
 
-    pltpu.make_async_copy(
-        got_b.at[pl.ds(0, HST - 1)], got_b.at[pl.ds(0, HST - 1)], recv_sem.at[4]
-    ).wait()
-    terms = got_b[...].astype(jnp.float32)
-    value, stat = terms[:, :8], terms[:, 8:]
-    turned = pltpu.roll(stat, HD // 2, 2)
-    low = lax.broadcasted_iota(jnp.int32, stat.shape, 2) < HD // 2
-    peaks = jnp.where(low, stat, turned)
-    sums = jnp.where(low, turned, stat)
-    factor = jnp.exp2(peaks - jnp.max(peaks, axis=0, keepdims=True))
-    attended = jnp.sum(factor * value, axis=0) / jnp.sum(factor * sums, axis=0)
-    att[pl.ds(me, 1)] = attended.astype(jnp.bfloat16)[None]
-
-    for d in plane_peers():
-        pltpu.make_async_remote_copy(
-            att.at[me], att.at[me], send_sem.at[6], recv_sem.at[5],
+    def send_c(d):
+        pltpu.make_async_remote_copy(
+            att.at[chip], att.at[chip], send_sem.at[6], recv_sem.at[5],
             device_id=at_hst(d), device_id_type=MESH,
         ).start()
+
+    @pl.when(core == 1)
+    def _():
+        pltpu.make_async_copy(
+            got_b.at[pl.ds(0, HST - 1)], got_b.at[pl.ds(0, HST - 1)], recv_sem.at[4]
+        ).wait()
+        terms = got_b[...].astype(jnp.float32)
+        value, stat = terms[:, :16], terms[:, 16:]
+        turned = pltpu.roll(stat, HD // 2, 2)
+        low = lax.broadcasted_iota(jnp.int32, stat.shape, 2) < HD // 2
+        peaks = jnp.where(low, stat, turned)
+        sums = jnp.where(low, turned, stat)
+        factor = jnp.exp2(peaks - jnp.max(peaks, axis=0, keepdims=True))
+        attended = jnp.sum(factor * value, axis=0) / jnp.sum(factor * sums, axis=0)
+        att[pl.ds(chip, 1)] = attended.astype(jnp.bfloat16)[None]
+
+        for c in other_chips():
+            send_c(c * 2)
+            send_c(c * 2 + 1)
+        send_c(mate)
 
     @pl.when(me > 0)
     def _():
@@ -306,27 +339,53 @@
     def _():
         pltpu.make_async_remote_copy(
             anchor.at[core], anchor.at[core], send_sem.at[4], recv_sem.at[3],
-            device_id=at_hst(me + 1 - 2 * core), device_id_type=MESH,
+            device_id=at_hst(mate), device_id_type=MESH,
         ).start()
 
     load_w.wait()
-    pltpu.make_async_copy(
-        att.at[pl.ds(0, HST - 1)], att.at[pl.ds(0, HST - 1)], recv_sem.at[5]
-    ).wait()
+
+    def landed(ref, n, sem):
+        pltpu.make_async_copy(ref.at[pl.ds(0, n)], ref.at[pl.ds(0, n)], sem).wait()
+
+    @pl.when(core == 0)
+    def _():
+        landed(att, CHIPS, recv_sem.at[5])
+
+    @pl.when(core == 1)
+    def _():
+        landed(att, CHIPS - 1, recv_sem.at[5])
+
     rows = att[...].astype(jnp.float32).reshape(HEADS, QN, HD)
     wide = jnp.concatenate([rows[h] for h in range(HEADS)], axis=1).astype(jnp.bfloat16)
-    partial = dot(wide, weight[...])
-    for t in range(TP):
+    partial = dot(wide, weight[...]).astype(jnp.bfloat16)
+    for t in range(TILES):
         r, c = t // 2, t % 2
-        part[t] = partial[r * 8 : r * 8 + 8, c * HD : (c + 1) * HD].astype(jnp.bfloat16)
-
-    for d in along_peers():
-        pltpu.make_async_remote_copy(
-            part.at[d], got_d.at[z], send_sem.at[7], recv_sem.at[6],
-            device_id=at_tp(d), device_id_type=MESH,
-        ).start()
-
-    got_d[pl.ds(z, 1)] = part[pl.ds(z, 1)]
+        part[t] = partial[r * 16 : r * 16 + 16, c * HD : (c + 1) * HD]
+
+    @pl.when(core == 1)
+    def _():
+        pl.semaphore_wait(barrier, 2 * TP - 1)
+        pl.semaphore_signal(ready.at[1], inc=1, device_id=at_hst(mate), device_id_type=MESH)
+
+    @pl.when(core == 0)
+    def _():
+        pl.semaphore_wait(ready.at[1], 1)
+
+    slot = core * TP + z
+    for t in (7, 6, 0, 5, 4, 3, 2, 1):
+        r = (FIRST + t) % TP
+
+        @pl.when((core == 0) | (z != r))
+        def _():
+            pltpu.make_async_remote_copy(
+                part.at[t], got_d.at[slot], send_sem.at[7], recv_sem.at[6],
+                device_id={"hst": column, "tp": r}, device_id_type=MESH,
+            ).start()
+
+        @pl.when((core == 1) & (z == r))
+        def _():
+            got_d[pl.ds(slot, 1)] = part[pl.ds(t, 1)]
+
     @pl.when(me > 0)
     def _():
         pltpu.make_async_copy(anchor.at[0], anchor.at[0], recv_sem.at[3]).wait()
@@ -334,41 +393,59 @@
     finish_head(0)
     finish_head(1)
 
-    pltpu.make_async_copy(
-        got_d.at[pl.ds(0, TP - 1)], got_d.at[pl.ds(0, TP - 1)], recv_sem.at[6]
-    ).wait()
-    total = jnp.sum(got_d[...].astype(jnp.float32), axis=0)
-    got_e[pl.ds(z, 1)] = total.astype(jnp.bfloat16)[None]
-
-    for d in along_peers():
-        pltpu.make_async_remote_copy(
-            got_e.at[z], got_e.at[z], send_sem.at[8], recv_sem.at[7],
-            device_id=at_tp(d), device_id_type=MESH,
-        ).start()
+    def send_e(src, where):
+        pltpu.make_async_remote_copy(
+            src, got_e.at[tile], send_sem.at[8], recv_sem.at[7],
+            device_id=where, device_id_type=MESH,
+        ).start()
+
+    @pl.when(adds)
+    def _():
+        landed(got_d, 2 * TP - 1, recv_sem.at[6])
+        total = got_d[...].astype(jnp.float32)
+        summed[...] = jnp.sum(total[:TP], axis=0).astype(jnp.bfloat16)
+        got_e[pl.ds(tile, 1)] = jnp.sum(total[TP:], axis=0).astype(jnp.bfloat16)[None]
+        for d in range(TP):
+            send_e(summed, {"hst": column - 1, "tp": d})
+
+            @pl.when(z != d)
+            def _():
+                send_e(got_e.at[tile], {"hst": column, "tp": d})
 
     finish_head(2)
     finish_head(3)
 
-    pltpu.make_async_copy(
-        got_e.at[pl.ds(0, TP - 1)], got_e.at[pl.ds(0, TP - 1)], recv_sem.at[7]
-    ).wait()
-    tiles = got_e[...].astype(jnp.float32)
-    query_out[...] = jnp.concatenate(
-        [
-            jnp.concatenate([tiles[2 * r], tiles[2 * r + 1]], axis=1)
-            for r in range(TP // 2)
-        ],
-        axis=0,
-    ).astype(jnp.bfloat16)
-
-    for sem, ref in (
-        (0, gather_q.at[pl.ds(0, HST - 1)]),
-        (5, got_b.at[pl.ds(0, HST - 1)]),
-        (6, att.at[pl.ds(0, HST - 1)]),
-        (7, got_d.at[pl.ds(0, TP - 1)]),
-        (8, got_e.at[pl.ds(0, TP - 1)]),
-    ):
-        pltpu.make_async_copy(ref, ref, send_sem.at[sem]).wait()
+    @pl.when(adds)
+    def _():
+        landed(got_e, TILES - 1, recv_sem.at[7])
+
+    @pl.when(jnp.logical_not(adds))
+    def _():
+        landed(got_e, TILES, recv_sem.at[7])
+
+    for t in range(TILES):
+        query_out[t // 2 * 16 : t // 2 * 16 + 16, t % 2 * HD : (t % 2 + 1) * HD] = got_e[t]
+
+    landed(gather_q, HST - 1, send_sem.at[0])
+
+    @pl.when(core == 0)
+    def _():
+        landed(sent_b, CHIPS, send_sem.at[5])
+        landed(part, TILES, send_sem.at[7])
+
+    @pl.when(core == 1)
+    def _():
+        landed(sent_b, CHIPS - 1, send_sem.at[5])
+        landed(got_d, 2 * CHIPS - 1, send_sem.at[6])
+
+    @pl.when(adds)
+    def _():
+        landed(part, TILES - 1, send_sem.at[7])
+        landed(got_d, 2 * TP - 1, send_sem.at[8])
+
+    @pl.when((core == 1) & (tile >= TILES))
+    def _():
+        landed(part, TILES, send_sem.at[7])
 
     def sent(sem, rows):
         ref = own.at[0, pl.ds(0, rows)]
@@ -418,15 +495,17 @@
             pltpu.VMEM((HEADS, ROWS, HD), f32),
             pltpu.VMEM((HST, 8, HD), bf16),
             pltpu.VMEM((HST * 8, HD), f32),
-            pltpu.VMEM((HST, 16, HD), bf16),
-            pltpu.VMEM((HST, 16, HD), bf16),
-            pltpu.VMEM((HST, 8, HD), bf16),
-            pltpu.VMEM((TP, 8, HD), bf16),
-            pltpu.VMEM((TP, 8, HD), bf16),
-            pltpu.VMEM((TP, 8, HD), bf16),
+            pltpu.VMEM((CHIPS, 32, HD), bf16),
+            pltpu.VMEM((HST, 32, HD), bf16),
+            pltpu.VMEM((CHIPS, 16, HD), bf16),
+            pltpu.VMEM((TILES, 16, HD), bf16),
+            pltpu.VMEM((2 * TP, 16, HD), bf16),
+            pltpu.VMEM((16, HD), bf16),
+            pltpu.VMEM((TILES, 16, HD), bf16),
             pltpu.SemaphoreType.DMA((7,)),
             pltpu.SemaphoreType.DMA((9,)),
             pltpu.SemaphoreType.DMA((8,)),
+            pltpu.SemaphoreType.REGULAR((2,)),
         ],
         compiler_params=pltpu.CompilerParams(
             collective_id=0, has_side_effects=True, vmem_limit_bytes=48 * 1024 * 1024

time: 48.8 us -> 43.8 us (0.90)
  Pallas kernels: 46.3 us -> 41.5 us
    pallas_call x1, Pallas kernels: 46.3 us -> 41.5 us  [per_device(): pl.pallas_call(kernel, out_shape=(pltpu.VMEM((ROWS, HEADS * HD), bf16), p...]
where the time goes in v3:
time: 43.8 us; the launch traced here: 43.6 us
  Pallas kernels  41.5 us (95%)
  local copies, waits for them, and re-layouts  1.5 us (3%)
  between operations  0.64 us (1%)
    pallas_call x1, Pallas kernels, per_device(): pl.pallas_call(kernel, out_shape=(pltpu.VMEM((ROWS, HEADS * HD), bf16), p...  41.5 us
    unnamed x2, local copies, waits for them, and re-layouts  1.5 us

profile of v3, /device:TPU:1, one launch (start us, length us, event | category | flops | bytes accessed | tf_op | source)
XLA Modules:
  0.0 43.6 jit_solution(10001198662626455493)
XLA Ops:
  0.6 41.5 %shard_map.77 = (bf16[768,512]{1,0:T(8,128)(2,1)S(1)}, bf16[64,256]{1,0:T(8,128)(2,1)S(1)}) custom-call(s32[32]{0:T(128)} %lengths_hbm.1, bf16[768,512]{1,0:T(8,128)(2,1)} %ctx_q.1, bf16[2,768,1024]{2,1,0:T(8,128)(2,1)} %ctx_kv.1, bf16[2,512]{1,0:T(2,128)(2,1)} %query_q.1, bf16[2,2,1024]{2,1,0:T(2,128)(2,1)} %query_kv.1, bf16[512,256]{1,0:T(8,128)(2,1)} %out_weight.1), custom_call_target="tpu_custom_call" | custom-call | tf_op jit(solution)/shard_map/pallas_call | solution.py:476
  42.1 0.9 %copy.10 = bf16[768,512]{1,0:T(8,128)(2,1)} copy(bf16[768,512]{1,0:T(8,128)(2,1)S(1)} %get-tuple-element.2) | data formatting | bytes 1572864
  43.0 0.6 %copy.11 = bf16[64,256]{1,0:T(8,128)(2,1)} copy(bf16[64,256]{1,0:T(8,128)(2,1)S(1)} %get-tuple-element.3) | data formatting | bytes 65536

commit v4 on v3

--- a/solution.py
+++ b/solution.py
@@ -27,7 +27,7 @@
     key=lambda o: -(min(o[0], 4 - o[0]) + min(o[1], 4 - o[1])),
 )
 TILES = 8
-FIRST = 11
+FIRST = 10
 
 
 def dot_t(a, b):
@@ -55,6 +55,7 @@
     cq,
     own,
     anchor,
+    values_piece,
     weight,
     qq,
     qkv,
@@ -63,6 +64,7 @@
     sum1,
     max1,
     gather_q,
+    handed_q,
     rows_q,
     sent_b,
     got_b,
@@ -102,22 +104,23 @@
     load_qkv = pltpu.make_async_copy(query_kv, qkv, local_sem.at[3])
     load_w = pltpu.make_async_copy(out_weight, weight, local_sem.at[4])
     load_len = pltpu.make_async_copy(lengths_hbm, lengths, local_sem.at[6])
-    for copy in (load_len, load_qq, load_kv, load_cq, load_qkv, load_w):
-        copy.start()
+    load_qq.start()
 
     barrier = pltpu.get_barrier_semaphore()
 
     def greet(**where):
         pl.semaphore_signal(barrier, inc=1, device_id=where, device_id_type=MESH)
 
-    for c in other_chips():
-        greet(hst=c * 2)
+    @pl.when(core == 0)
+    def _():
+        for c in other_chips():
+            greet(hst=c * 2)
+
+    greet(hst=mate)
+    for copy in (load_kv, load_cq, load_len, load_qkv, load_w):
+        copy.start()
     for dz in (8, 7, 9, 6, 10, 5, 11, 4, 12, 3, 13, 2, 14, 1, 15):
         greet(hst=column, tp=lax.rem(z + dz, TP))
-    greet(hst=mate)
-
-    load_len.wait()
-    own_len = lengths[me]
 
     diag_row = lax.broadcasted_iota(jnp.int32, (TILE, TILE), 0)
     diag_col = lax.broadcasted_iota(jnp.int32, (TILE, TILE), 1)
@@ -138,6 +141,7 @@
             max1[h, rows, :] = jnp.broadcast_to(m, (TILE, HD))
 
     def live(rb, value):
+        own_len = lengths[me]
         rid = rb * TILE + lax.broadcasted_iota(jnp.int32, (TILE, HD), 0)
         return jnp.where(rid < own_len, value, 0.0).astype(jnp.bfloat16)
 
@@ -177,7 +181,7 @@
 
     @pl.when(core == 0)
     def _():
-        pl.semaphore_wait(barrier, HST - 1)
+        pl.semaphore_wait(barrier, CHIPS)
         pl.semaphore_signal(ready.at[0], inc=1, device_id=at_hst(mate), device_id_type=MESH)
 
     @pl.when(core == 1)
@@ -192,8 +196,10 @@
 
     for c in other_chips():
         send_a(c * 2)
-        send_a(c * 2 + 1)
-    send_a(mate)
+
+    @pl.when(core == 1)
+    def _():
+        send_a(mate)
 
     def piece(ref, plane, c):
         return ref.at[plane, pl.ds(pl.multiple_of(c * PIECE, 16), PIECE), :]
@@ -209,8 +215,8 @@
                 device_id=at_hst(c * 2), device_id_type=MESH,
             ).start()
             pltpu.make_async_remote_copy(
-                piece(own, 1, c), piece(anchor, 1, c), send_sem.at[2], recv_sem.at[1],
-                device_id=at_hst(c * 2 + 1), device_id_type=MESH,
+                piece(own, 1, c), values_piece, send_sem.at[2], recv_sem.at[9],
+                device_id=at_hst(c * 2), device_id_type=MESH,
             ).start()
 
         pltpu.make_async_remote_copy(
@@ -234,10 +240,26 @@
     for h in range(HEADS):
         own_head(h)
 
-    pltpu.make_async_copy(
-        gather_q.at[pl.ds(0, HST - 1)], gather_q.at[pl.ds(0, HST - 1)], recv_sem.at[0]
-    ).wait()
-    rows_q[...] = gather_q[...].astype(jnp.float32).reshape(HST * 8, HD)
+    def landed(ref, n, sem):
+        pltpu.make_async_copy(ref.at[pl.ds(0, n)], ref.at[pl.ds(0, n)], sem).wait()
+
+    hand_over = pltpu.make_async_remote_copy(
+        gather_q, handed_q, send_sem.at[9], recv_sem.at[8],
+        device_id=at_hst(mate), device_id_type=MESH,
+    )
+
+    @pl.when(core == 0)
+    def _():
+        landed(gather_q, HST - 1, recv_sem.at[0])
+        hand_over.start()
+        rows_q[...] = gather_q[...].astype(jnp.float32).reshape(HST * 8, HD)
+
+    @pl.when(core == 1)
+    def _():
+        hand_over.wait_recv()
+        rows_q[...] = handed_q[...].astype(jnp.float32).reshape(HST * 8, HD)
+
+    load_len.wait()
     q_all = jnp.concatenate(
         [rows_q[pl.ds(h, QN, stride=HEADS), :] for h in range(HEADS)], axis=0
     ).astype(jnp.bfloat16)
@@ -247,6 +269,7 @@
         selfkv[plane] = jnp.concatenate(
             [tiny, jnp.zeros((HD - 2, HD), jnp.float32)], axis=0
         ).astype(jnp.bfloat16)
+    own_len = lengths[me]
     s_ctx = dot_t(q_all, own[0])
     s_ctx = jnp.where(
         lax.broadcasted_iota(jnp.int32, s_ctx.shape, 1) < own_len, s_ctx, MASKED
@@ -285,6 +308,14 @@
     def _():
         got_b[pl.ds(me, 1)] = sent_b[pl.ds(chip, 1)]
 
+    @pl.when((me > 0) & (core == 0))
+    def _():
+        pltpu.make_async_copy(values_piece, values_piece, recv_sem.at[9]).wait()
+        pltpu.make_async_remote_copy(
+            values_piece, piece(anchor, 1, chip), send_sem.at[1], recv_sem.at[1],
+            device_id=at_hst(mate), device_id_type=MESH,
+        ).start()
+
     @pl.when(me > 0)
     def _():
         pltpu.make_async_copy(
@@ -325,8 +356,9 @@
         att[pl.ds(chip, 1)] = attended.astype(jnp.bfloat16)[None]
 
         for c in other_chips():
+            send_c(c * 2 + 1)
+        for c in other_chips():
             send_c(c * 2)
-            send_c(c * 2 + 1)
         send_c(mate)
 
     @pl.when(me > 0)
@@ -343,9 +375,6 @@
         ).start()
 
     load_w.wait()
-
-    def landed(ref, n, sem):
-        pltpu.make_async_copy(ref.at[pl.ds(0, n)], ref.at[pl.ds(0, n)], sem).wait()
 
     @pl.when(core == 0)
     def _():
@@ -406,12 +435,13 @@
         summed[...] = jnp.sum(total[:TP], axis=0).astype(jnp.bfloat16)
         got_e[pl.ds(tile, 1)] = jnp.sum(total[TP:], axis=0).astype(jnp.bfloat16)[None]
         for d in range(TP):
-            send_e(summed, {"hst": column - 1, "tp": d})
 
             @pl.when(z != d)
             def _():
                 send_e(got_e.at[tile], {"hst": column, "tp": d})
 
+            send_e(summed, {"hst": column - 1, "tp": d})
+
     finish_head(2)
     finish_head(3)
 
@@ -426,15 +456,16 @@
     for t in range(TILES):
         query_out[t // 2 * 16 : t // 2 * 16 + 16, t % 2 * HD : (t % 2 + 1) * HD] = got_e[t]
 
-    landed(gather_q, HST - 1, send_sem.at[0])
-
-    @pl.when(core == 0)
-    def _():
+    @pl.when(core == 0)
+    def _():
+        landed(gather_q, CHIPS - 1, send_sem.at[0])
+        hand_over.wait_send()
         landed(sent_b, CHIPS, send_sem.at[5])
         landed(part, TILES, send_sem.at[7])
 
     @pl.when(core == 1)
     def _():
+        landed(gather_q, CHIPS, send_sem.at[0])
         landed(sent_b, CHIPS - 1, send_sem.at[5])
         landed(got_d, 2 * CHIPS - 1, send_sem.at[6])
 
@@ -456,6 +487,10 @@
         sent(1, ROWS - PIECE)
         sent(2, ROWS)
 
+    @pl.when((me > 0) & (core == 0))
+    def _():
+        sent(1, PIECE)
+
     @pl.when(core + (me == 0) > 0)
     def _():
         sent(3, ROWS - PIECE)
@@ -467,13 +502,24 @@
     @pl.when((me == 0) | (me > 1))
     def _():
         sent(4, ROWS)
+
+
+def save(ctx_in, query_in, ctx_out, query_out, sems):
+    copies = (
+        pltpu.make_async_copy(ctx_in, ctx_out, sems.at[0]),
+        pltpu.make_async_copy(query_in, query_out, sems.at[1]),
+    )
+    for copy in copies:
+        copy.start()
+    for copy in copies:
+        copy.wait()
 
 
 def per_device(ctx_q, ctx_kv, lengths, query_q, query_kv, out_weight):
     bf16, f32 = jnp.bfloat16, jnp.float32
     hbm = pl.BlockSpec(memory_space=pltpu.HBM)
     vmem = pl.BlockSpec(memory_space=pltpu.VMEM)
-    return pl.pallas_call(
+    outs = pl.pallas_call(
         kernel,
         out_shape=(
             pltpu.VMEM((ROWS, HEADS * HD), bf16),
@@ -486,6 +532,7 @@
             pltpu.VMEM((ROWS, HEADS * HD), bf16),
             pltpu.VMEM((2, ROWS, HD), bf16),
             pltpu.VMEM((2, ROWS, HD), bf16),
+            pltpu.VMEM((PIECE, HD), bf16),
             pltpu.VMEM((HEADS * HD, COLS), bf16),
             pltpu.VMEM((2, HEADS * HD), bf16),
             pltpu.VMEM((2, 2, KVH * HD), bf16),
@@ -493,6 +540,7 @@
             pltpu.VMEM((HEADS, ROWS, HD), f32),
             pltpu.VMEM((HEADS, ROWS, HD), f32),
             pltpu.VMEM((HEADS, ROWS, HD), f32),
+            pltpu.VMEM((HST, 8, HD), bf16),
             pltpu.VMEM((HST, 8, HD), bf16),
             pltpu.VMEM((HST * 8, HD), f32),
             pltpu.VMEM((CHIPS, 32, HD), bf16),
@@ -503,14 +551,27 @@
             pltpu.VMEM((16, HD), bf16),
             pltpu.VMEM((TILES, 16, HD), bf16),
             pltpu.SemaphoreType.DMA((7,)),
-            pltpu.SemaphoreType.DMA((9,)),
-            pltpu.SemaphoreType.DMA((8,)),
+            pltpu.SemaphoreType.DMA((10,)),
+            pltpu.SemaphoreType.DMA((10,)),
             pltpu.SemaphoreType.REGULAR((2,)),
         ],
         compiler_params=pltpu.CompilerParams(
             collective_id=0, has_side_effects=True, vmem_limit_bytes=48 * 1024 * 1024
         ),
     )(*(pltpu.with_memory_space_constraint(a, pltpu.HBM) for a in (lengths, ctx_q, ctx_kv, query_q, query_kv, out_weight)))
+
+
+    any_space = pl.BlockSpec(memory_space=pl.ANY)
+    return pl.pallas_call(
+        save,
+        out_shape=(
+            jax.ShapeDtypeStruct((ROWS, HEADS * HD), bf16),
+            jax.ShapeDtypeStruct((QN, COLS), bf16),
+        ),
+        in_specs=[any_space] * 2,
+        out_specs=(any_space, any_space),
+        scratch_shapes=[pltpu.SemaphoreType.DMA((2,))],
+    )(*(pltpu.with_memory_space_constraint(a, pltpu.VMEM) for a in outs))
 
 
 def solution(mesh):

time: 43.8 us -> 42.7 us (0.975)
  local copies, waits for them, and re-layouts: 1.5 us -> 0 us
    unnamed x2 -> x0, local copies, waits for them, and re-layouts: 1.5 us -> none
    pallas_call x0 -> x1, Pallas kernels: none -> 0.9 us  [per_device(): pl.pallas_call(save, out_shape=(jax.ShapeDtypeStruct((ROWS, HEADS * HD),...]
    pallas_call x1, Pallas kernels: 41.5 us -> 41 us  [per_device(): pl.pallas_call(kernel, out_shape=(pltpu.VMEM((ROWS, HEADS * HD), bf16), p...]
where the time goes in v4:
time: 42.7 us; the launch traced here: 42.6 us
  Pallas kernels  41.9 us (98%)
  between operations  0.64 us (1%)
    pallas_call x1, Pallas kernels, per_device(): pl.pallas_call(kernel, out_shape=(pltpu.VMEM((ROWS, HEADS * HD), bf16), p...  41 us
    pallas_call x1, Pallas kernels, per_device(): pl.pallas_call(save, out_shape=(jax.ShapeDtypeStruct((ROWS, HEADS * HD),...  0.9 us

profile of v4, /device:TPU:1, one launch (start us, length us, event | category | flops | bytes accessed | tf_op | source)
XLA Modules:
  0.0 42.6 jit_solution(16113715364221259857)
XLA Ops:
  0.6 41.0 %shard_map.77 = (bf16[768,512]{1,0:T(8,128)(2,1)S(1)}, bf16[64,256]{1,0:T(8,128)(2,1)S(1)}) custom-call(s32[32]{0:T(128)} %lengths_hbm.1, bf16[768,512]{1,0:T(8,128)(2,1)} %ctx_q.1, bf16[2,768,1024]{2,1,0:T(8,128)(2,1)} %ctx_kv.1, bf16[2,512]{1,0:T(2,128)(2,1)} %query_q.1, bf16[2,2,1024]{2,1,0:T(2,128)(2,1)} %query_kv.1, bf16[512,256]{1,0:T(8,128)(2,1)} %out_weight.1), custom_call_target="tpu_custom_call" | custom-call | tf_op jit(solution)/shard_map/pallas_call | solution.py:522
  41.6 0.9 %shard_map.78 = (bf16[768,512]{1,0:T(8,128)(2,1)}, bf16[64,256]{1,0:T(8,128)(2,1)}) custom-call(bf16[768,512]{1,0:T(8,128)(2,1)S(1)} %get-tuple-element.4.ctx_in, bf16[64,256]{1,0:T(8,128)(2,1)S(1)} %get-tuple-element.5.query_in), custom_call_target="tpu_custom_call" | custom-call | tf_op jit(solution)/shard_map/pallas_call | solution.py:565

commit v5 on v4

v5 whole, which is shorter than its diff:
```python
import jax
import jax.numpy as jnp
from jax import lax
from jax.experimental import pallas as pl
from jax.experimental.pallas import tpu as pltpu
from jax.sharding import PartitionSpec as P

H = 64
KVH = 8
HD = 128
HST = 32
TP = 16
ROWS = 768
HEADS = H // TP
TILE = 256
CHIPS = HST // 2
PIECE = ROWS // CHIPS
QN = 64
COLS = 256
MASKED = -1e30
SCALE2 = HD ** (-0.5) * 1.4426950408889634
MESH = pl.DeviceIdType.MESH


SLOTS = sorted(
    [(y, x) for y in range(4) for x in range(4)],
    key=lambda o: min(o[0], 4 - o[0]) + min(o[1], 4 - o[1]),
)
CHIP_OFFSETS = SLOTS[:0:-1]
GROUPS = ((0, 5), (5, 11), (11, 16))
A_SEMS = (0, 9, 10)
TILES = 8
ADDERS = (10, 11, 12, 13, 14, 15, 1, 2)
HIGH = 10
LOW = 1


def dot_t(a, b):
    return lax.dot_general(a, b, (((1,), (1,)), ((), ())), preferred_element_type=jnp.float32)


def dot(a, b):
    return jnp.dot(a, b, preferred_element_type=jnp.float32)


def with_ones(values):
    return jnp.concatenate([values, jnp.ones_like(values)], axis=1)


def kernel(
    lengths_hbm,
    ctx_q,
    ctx_kv,
    query_q,
    query_kv,
    out_weight,
    ctx_out,
    query_out,
    lengths,
    cq,
    own,
    anchor,
    weight,
    qq,
    qkv,
    selfkv,
    out1,
    sum1,
    max1,
    gather_q,
    rows_f,
    sent_b,
    got_b,
    att,
    part,
    got_d,
    summed,
    got_e,
    local_sem,
    send_sem,
    recv_sem,
    ready,
):
    me = lax.axis_index("hst")
    z = lax.axis_index("tp")
    chip = me // 2
    core = lax.rem(me, 2)
    kv_off = pl.multiple_of((z // 2) * HD, HD)

    py, px = chip // 4, lax.rem(chip, 4)

    mate = me + 1 - 2 * core
    column = chip * 2 + 1
    tile = jnp.where(z >= HIGH, z - HIGH, z - LOW + TP - HIGH)
    chosen = (z >= HIGH) | ((z >= LOW) & (z < LOW + TILES - TP + HIGH))
    adds = (core == 1) & chosen

    def chip_at(dy, dx):
        return lax.rem(py + dy + 4, 4) * 4 + lax.rem(px + dx + 4, 4)

    def other_chips():
        for dy, dx in CHIP_OFFSETS:
            yield chip_at(dy, dx)

    def at_hst(d):
        return {"hst": d}

    load_kv = pltpu.make_async_copy(ctx_kv.at[:, :, pl.ds(kv_off, HD)], own, local_sem.at[0])
    load_cq = pltpu.make_async_copy(ctx_q, cq, local_sem.at[1])
    load_qq = pltpu.make_async_copy(query_q, qq, local_sem.at[2])
    load_qkv = pltpu.make_async_copy(query_kv, qkv, local_sem.at[3])
    load_w = pltpu.make_async_copy(out_weight, weight, local_sem.at[4])
    load_len = pltpu.make_async_copy(lengths_hbm, lengths, local_sem.at[6])
    load_qq.start()

    barrier = pltpu.get_barrier_semaphore()

    def greet(**where):
        pl.semaphore_signal(barrier, inc=1, device_id=where, device_id_type=MESH)

    for c in other_chips():
        greet(hst=c * 2)
    greet(hst=mate)
    for copy in (load_kv, load_cq, load_len, load_qkv, load_w):
        copy.start()
    for dz in (8, 7, 9, 6, 10, 5, 11, 4, 12, 3, 13, 2, 14, 1, 15):
        greet(hst=column, tp=lax.rem(z + dz, TP))

    diag_row = lax.broadcasted_iota(jnp.int32, (TILE, TILE), 0)
    diag_col = lax.broadcasted_iota(jnp.int32, (TILE, TILE), 1)

    def own_head(h):
        cols = pl.ds(pl.multiple_of(h * HD, HD), HD)
        for rb in range(ROWS // TILE):
            rows = pl.ds(rb * TILE, TILE)
            q = cq[rows, cols]
            keys = (rb + 1) * TILE
            s = dot_t(q, own[0, 0:keys, :])
            last = jnp.where(diag_col <= diag_row, s[:, keys - TILE :], MASKED)
            s = last if rb == 0 else jnp.concatenate([s[:, : keys - TILE], last], axis=1)
            m = jnp.max(s, axis=1, keepdims=True) * SCALE2
            p = jnp.exp2(s * SCALE2 - m).astype(jnp.bfloat16)
            o = dot(p, with_ones(own[1, 0:keys, :]))
            out1[h, rows, :] = o[:, :HD]
            sum1[h, rows, :] = o[:, HD:]
            max1[h, rows, :] = jnp.broadcast_to(m, (TILE, HD))

    def live(rb, value):
        own_len = lengths[me]
        rid = rb * TILE + lax.broadcasted_iota(jnp.int32, (TILE, HD), 0)
        return jnp.where(rid < own_len, value, 0.0).astype(jnp.bfloat16)

    def anchor_head(h):
        cols = pl.ds(pl.multiple_of(h * HD, HD), HD)
        for rb in range(ROWS // TILE):
            rows = pl.ds(rb * TILE, TILE)
            q = cq[rows, cols]
            s = dot_t(q, anchor[0])
            before = max1[h, rows, :]
            m = jnp.maximum(jnp.max(s, axis=1, keepdims=True) * SCALE2, before[:, :1])
            p = jnp.exp2(s * SCALE2 - m).astype(jnp.bfloat16)
            o = dot(p, with_ones(anchor[1]))
            keep = jnp.exp2(before - m)
            num = out1[h, rows, :] * keep + o[:, :HD]
            den = sum1[h, rows, :] * keep + o[:, HD:]
            ctx_out[rows, cols] = live(rb, num / den)

    def first_head(h):
        cols = pl.ds(pl.multiple_of(h * HD, HD), HD)
        for rb in range(ROWS // TILE):
            rows = pl.ds(rb * TILE, TILE)
            ctx_out[rows, cols] = live(rb, out1[h, rows, :] / sum1[h, rows, :])

    def finish_head(h):
        @pl.when(me > 0)
        def _():
            anchor_head(h)

        @pl.when(me == 0)
        def _():
            first_head(h)

    load_qq.wait()
    mine = qq[...].astype(jnp.float32)
    gather_q[pl.ds(core, 1)] = jnp.concatenate(
        [mine[t : t + 1, h * HD : (h + 1) * HD] for t in range(2) for h in range(HEADS)], axis=0
    ).astype(jnp.bfloat16)[None]

    @pl.when(core == 0)
    def _():
        pl.semaphore_wait(barrier, HST - 1)
        pl.semaphore_signal(ready.at[0], inc=1, device_id=at_hst(mate), device_id_type=MESH)

    @pl.when(core == 1)
    def _():
        pl.semaphore_wait(ready.at[0], 1)

    def send_a(d, k, group):
        pltpu.make_async_remote_copy(
            gather_q.at[core], gather_q.at[2 * k + core], send_sem.at[0],
            recv_sem.at[A_SEMS[group]], device_id=at_hst(d), device_id_type=MESH,
        ).start()

    for group in (2, 1, 0):
        for k in reversed(range(*GROUPS[group])):
            if k:
                send_a(chip_at(*SLOTS[k]) * 2, k, group)
                send_a(chip_at(*SLOTS[k]) * 2 + 1, k, group)
    send_a(mate, 0, 0)

    def piece(ref, plane, c):
        return ref.at[plane, pl.ds(pl.multiple_of(c * PIECE, 16), PIECE), :]

    load_kv.wait()

    @pl.when(me == 0)
    def _():
        @pl.loop(1, CHIPS)
        def _(c):
            pltpu.make_async_remote_copy(
                piece(own, 0, c), piece(anchor, 0, c), send_sem.at[1], recv_sem.at[1],
                device_id=at_hst(c * 2), device_id_type=MESH,
            ).start()
            pltpu.make_async_remote_copy(
                piece(own, 1, c), piece(anchor, 1, c), send_sem.at[2], recv_sem.at[1],
                device_id=at_hst(c * 2 + 1), device_id_type=MESH,
            ).start()

        pltpu.make_async_remote_copy(
            piece(own, 1, 0), piece(anchor, 1, 0), send_sem.at[2], recv_sem.at[1],
            device_id=at_hst(1), device_id_type=MESH,
        ).start()

        @pl.loop(1, CHIPS)
        def _(c):
            pltpu.make_async_remote_copy(
                piece(own, 0, 0), piece(anchor, 0, 0), send_sem.at[3], recv_sem.at[2],
                device_id=at_hst(c * 2), device_id_type=MESH,
            ).start()

        pltpu.make_async_remote_copy(
            own.at[0], anchor.at[0], send_sem.at[4], recv_sem.at[3],
            device_id=at_hst(1), device_id_type=MESH,
        ).start()

    load_cq.wait()
    first = jnp.where(me == 0, 0, 2)
    pl.loop(0, first)(own_head)

    def landed(ref, n, sem):
        pltpu.make_async_copy(ref.at[pl.ds(0, n)], ref.at[pl.ds(0, n)], sem).wait()

    load_len.wait()
    load_qkv.wait()
    for plane in range(2):
        tiny = qkv[plane, :, pl.ds(kv_off, HD)].astype(jnp.float32)
        selfkv[plane] = jnp.concatenate(
            [tiny, jnp.zeros((HD - 2, HD), jnp.float32)], axis=0
        ).astype(jnp.bfloat16)
    own_len = lengths[me]
    quarter = lax.shift_right_logical(lax.broadcasted_iota(jnp.int32, (16, HD), 0), 2)

    def query_terms(lo, hi):
        n = (hi - lo) * 16
        q = gather_q[2 * lo : 2 * hi].astype(jnp.float32).reshape(n, HD).astype(jnp.bfloat16)
        s_ctx = dot_t(q, own[0])
        s_ctx = jnp.where(
            lax.broadcasted_iota(jnp.int32, s_ctx.shape, 1) < own_len, s_ctx, MASKED
        )
        s_self = dot_t(q, selfkv[0])
        token = jnp.concatenate(
            [chip_at(-SLOTS[k][0], -SLOTS[k][1]) * 4 + quarter for k in range(lo, hi)], axis=0
        )
        key = lax.broadcasted_iota(jnp.int32, s_self.shape, 1)
        s_self = jnp.where((key < 2) & (me * 2 + key <= token), s_self, MASKED)
        peak = jnp.maximum(
            jnp.max(s_ctx, axis=1, keepdims=True), jnp.max(s_self, axis=1, keepdims=True)
        )
        peak = (peak * SCALE2).astype(jnp.bfloat16).astype(jnp.float32)
        p_ctx = jnp.exp2(s_ctx * SCALE2 - peak).astype(jnp.bfloat16)
        p_self = jnp.exp2(s_self * SCALE2 - peak).astype(jnp.bfloat16)
        o = dot(p_ctx, with_ones(own[1])) + dot(p_self, with_ones(selfkv[1]))
        lane = lax.broadcasted_iota(jnp.int32, (n, HD), 1)
        stats = jnp.where(lane < HD // 2, jnp.broadcast_to(peak, (n, HD)), o[:, HD:])
        sent_b[lo:hi] = jnp.concatenate(
            [o[:, :HD].reshape(hi - lo, 16, HD), stats.reshape(hi - lo, 16, HD)], axis=1
        ).astype(jnp.bfloat16)

    def send_b(k, d):
        pltpu.make_async_remote_copy(
            sent_b.at[k], got_b.at[me], send_sem.at[5], recv_sem.at[4],
            device_id=at_hst(d), device_id_type=MESH,
        ).start()

    for group, (lo, hi) in enumerate(GROUPS):
        landed(gather_q, 2 * (hi - lo) - (group == 0), recv_sem.at[A_SEMS[group]])
        query_terms(lo, hi)
        for k in range(lo, hi):
            dy, dx = SLOTS[k]
            if k < CHIPS - 1:
                send_b(k, chip_at(2 - dy, 2 - dx) * 2 + 1)

    @pl.when(core == 0)
    def _():
        send_b(CHIPS - 1, mate)

    @pl.when(core == 1)
    def _():
        got_b[pl.ds(me, 1)] = sent_b[CHIPS - 1 : CHIPS]

    pl.loop(first, HEADS)(own_head)
    opposite = chip_at(2, 2)

    def send_c(d):
        pltpu.make_async_remote_copy(
            att.at[opposite], att.at[opposite], send_sem.at[6], recv_sem.at[5],
            device_id=at_hst(d), device_id_type=MESH,
        ).start()

    @pl.when(core == 1)
    def _():
        pltpu.make_async_copy(
            got_b.at[pl.ds(0, HST - 1)], got_b.at[pl.ds(0, HST - 1)], recv_sem.at[4]
        ).wait()
        terms = got_b[...].astype(jnp.float32)
        value, stat = terms[:, :16], terms[:, 16:]
        turned = pltpu.roll(stat, HD // 2, 2)
        low = lax.broadcasted_iota(jnp.int32, stat.shape, 2) < HD // 2
        peaks = jnp.where(low, stat, turned)
        sums = jnp.where(low, turned, stat)
        factor = jnp.exp2(peaks - jnp.max(peaks, axis=0, keepdims=True))
        attended = jnp.sum(factor * value, axis=0) / jnp.sum(factor * sums, axis=0)
        att[pl.ds(opposite, 1)] = attended.astype(jnp.bfloat16)[None]

        for c in other_chips():
            send_c(c * 2 + 1)
        for c in other_chips():
            send_c(c * 2)
        send_c(mate)

    @pl.when(me > 0)
    def _():
        pltpu.make_async_copy(
            piece(anchor, 0, 0), piece(anchor, 0, 0), recv_sem.at[1]
        ).wait()

        @pl.loop(1, CHIPS)
        def _(k):
            c = lax.rem(chip + k, CHIPS)

            @pl.when(c * 2 + core > 0)
            def _():
                pltpu.make_async_remote_copy(
                    piece(anchor, core, chip), piece(anchor, core, chip),
                    send_sem.at[3], recv_sem.at[2],
                    device_id=at_hst(c * 2 + core), device_id_type=MESH,
                ).start()

    load_w.wait()

    @pl.when(core == 0)
    def _():
        landed(att, CHIPS, recv_sem.at[5])

    @pl.when(core == 1)
    def _():
        landed(att, CHIPS - 1, recv_sem.at[5])

    rows_f[...] = att[...].astype(jnp.float32).reshape(HST * 8, HD)
    wide = jnp.concatenate(
        [rows_f[pl.ds(h, QN, stride=HEADS), :] for h in range(HEADS)], axis=1
    ).astype(jnp.bfloat16)
    partial = dot(wide, weight[...]).astype(jnp.bfloat16)
    for t in range(TILES):
        r, c = t // 2, t % 2
        part[t] = partial[r * 16 : r * 16 + 16, c * HD : (c + 1) * HD]

    @pl.when(core == 1)
    def _():
        pl.semaphore_wait(barrier, 2 * TP - 1)
        pl.semaphore_signal(ready.at[1], inc=1, device_id=at_hst(mate), device_id_type=MESH)

    @pl.when(core == 0)
    def _():
        pl.semaphore_wait(ready.at[1], 1)

    for t in (7, 6, 0, 5, 4, 3, 2, 1):
        r = ADDERS[t]

        @pl.when((core == 0) | (z != r))
        def _():
            pltpu.make_async_remote_copy(
                part.at[t], got_d.at[core, z], send_sem.at[7], recv_sem.at[6 + core],
                device_id={"hst": column, "tp": r}, device_id_type=MESH,
            ).start()

        @pl.when((core == 1) & (z == r))
        def _():
            got_d[1, pl.ds(z, 1)] = part[pl.ds(t, 1)]

    @pl.when(me > 0)
    def _():
        pltpu.make_async_copy(
            anchor.at[0, pl.ds(0, ROWS - PIECE)], anchor.at[0, pl.ds(0, ROWS - PIECE)], recv_sem.at[2]
        ).wait()

    @pl.when(me > 1)
    def _():
        pltpu.make_async_remote_copy(
            anchor.at[core], anchor.at[core], send_sem.at[4], recv_sem.at[3],
            device_id=at_hst(mate), device_id_type=MESH,
        ).start()

    @pl.when(me > 0)
    def _():
        pltpu.make_async_copy(anchor.at[0], anchor.at[0], recv_sem.at[3]).wait()

    early = jnp.where(z < TP // 2, HEADS, 0)
    pl.loop(0, early)(finish_head)

    def send_e(src, d, core_to):
        pltpu.make_async_remote_copy(
            src, got_e.at[tile], send_sem.at[8], recv_sem.at[8],
            device_id={"hst": column - 1 + core_to, "tp": d}, device_id_type=MESH,
        ).start()

    @pl.when(adds)
    def _():
        landed(got_d.at[1], TP - 1, recv_sem.at[7])
        total = jnp.sum(got_d[1].astype(jnp.float32), axis=0)
        got_e[pl.ds(tile, 1)] = total.astype(jnp.bfloat16)[None]
        for d in range(TP):

            @pl.when(z != d)
            def _():
                send_e(got_e.at[tile], d, 1)

        landed(got_d.at[0], TP, recv_sem.at[6])
        total = jnp.sum(got_d[0].astype(jnp.float32), axis=0)
        summed[...] = total.astype(jnp.bfloat16)
        for d in range(TP):
            send_e(summed, d, 0)

    pl.loop(early, HEADS)(finish_head)

    @pl.when(adds)
    def _():
        landed(got_e, TILES - 1, recv_sem.at[8])

    @pl.when(jnp.logical_not(adds))
    def _():
        landed(got_e, TILES, recv_sem.at[8])

    for t in range(TILES):
        query_out[t // 2 * 16 : t // 2 * 16 + 16, t % 2 * HD : (t % 2 + 1) * HD] = got_e[t]

    landed(gather_q, HST - 1, send_sem.at[0])
    @pl.when(core == 0)
    def _():
        landed(sent_b, CHIPS, send_sem.at[5])
        landed(part, TILES, send_sem.at[7])

    @pl.when(core == 1)
    def _():
        landed(sent_b, CHIPS - 1, send_sem.at[5])
        landed(got_d.at[0], TP, send_sem.at[6])
        landed(got_d.at[0], TP - 1, send_sem.at[6])

    @pl.when(adds)
    def _():
        landed(part, TILES - 1, send_sem.at[7])
        landed(got_d.at[0], TP, send_sem.at[8])
        landed(got_d.at[0], TP - 1, send_sem.at[8])

    @pl.when((core == 1) & jnp.logical_not(chosen))
    def _():
        landed(part, TILES, send_sem.at[7])

    def sent(sem, rows):
        ref = own.at[0, pl.ds(0, rows)]
        pltpu.make_async_copy(ref, ref, send_sem.at[sem]).wait()

    @pl.when(me == 0)
    def _():
        sent(1, ROWS - PIECE)
        sent(2, ROWS)

    @pl.when(core + (me == 0) > 0)
    def _():
        sent(3, ROWS - PIECE)

    @pl.when(core + (me == 0) == 0)
    def _():
        sent(3, ROWS - 2 * PIECE)

    @pl.when((me == 0) | (me > 1))
    def _():
        sent(4, ROWS)


def save(ctx_in, query_in, ctx_out, query_out, sems):
    copies = (
        pltpu.make_async_copy(ctx_in, ctx_out, sems.at[0]),
        pltpu.make_async_copy(query_in, query_out, sems.at[1]),
    )
    for copy in copies:
        copy.start()
    for copy in copies:
        copy.wait()


def per_device(ctx_q, ctx_kv, lengths, query_q, query_kv, out_weight):
    bf16, f32 = jnp.bfloat16, jnp.float32
    hbm = pl.BlockSpec(memory_space=pltpu.HBM)
    vmem = pl.BlockSpec(memory_space=pltpu.VMEM)
    outs = pl.pallas_call(
        kernel,
        out_shape=(
            pltpu.VMEM((ROWS, HEADS * HD), bf16),
            pltpu.VMEM((QN, COLS), bf16),
        ),
        in_specs=[hbm] * 6,
        out_specs=(vmem, vmem),
        scratch_shapes=[
            pltpu.SMEM((HST,), jnp.int32),
            pltpu.VMEM((ROWS, HEADS * HD), bf16),
            pltpu.VMEM((2, ROWS, HD), bf16),
            pltpu.VMEM((2, ROWS, HD), bf16),
            pltpu.VMEM((HEADS * HD, COLS), bf16),
            pltpu.VMEM((2, HEADS * HD), bf16),
            pltpu.VMEM((2, 2, KVH * HD), bf16),
            pltpu.VMEM((2, HD, HD), bf16),
            pltpu.VMEM((HEADS, ROWS, HD), f32),
            pltpu.VMEM((HEADS, ROWS, HD), f32),
            pltpu.VMEM((HEADS, ROWS, HD), f32),
            pltpu.VMEM((HST, 8, HD), bf16),
            pltpu.VMEM((HST * 8, HD), f32),
            pltpu.VMEM((CHIPS, 32, HD), bf16),
            pltpu.VMEM((HST, 32, HD), bf16),
            pltpu.VMEM((CHIPS, 16, HD), bf16),
            pltpu.VMEM((TILES, 16, HD), bf16),
            pltpu.VMEM((2, TP, 16, HD), bf16),
            pltpu.VMEM((16, HD), bf16),
            pltpu.VMEM((TILES, 16, HD), bf16),
            pltpu.SemaphoreType.DMA((7,)),
            pltpu.SemaphoreType.DMA((10,)),
            pltpu.SemaphoreType.DMA((11,)),
            pltpu.SemaphoreType.REGULAR((2,)),
        ],
        compiler_params=pltpu.CompilerParams(
            collective_id=0, has_side_effects=True, vmem_limit_bytes=48 * 1024 * 1024
        ),
    )(*(pltpu.with_memory_space_constraint(a, pltpu.HBM) for a in (lengths, ctx_q, ctx_kv, query_q, query_kv, out_weight)))


    any_space = pl.BlockSpec(memory_space=pl.ANY)
    return pl.pallas_call(
        save,
        out_shape=(
            jax.ShapeDtypeStruct((ROWS, HEADS * HD), bf16),
            jax.ShapeDtypeStruct((QN, COLS), bf16),
        ),
        in_specs=[any_space] * 2,
        out_specs=(any_space, any_space),
        scratch_shapes=[pltpu.SemaphoreType.DMA((2,))],
    )(*(pltpu.with_memory_space_constraint(a, pltpu.VMEM) for a in outs))


def solution(mesh):
    return jax.shard_map(
        per_device,
        mesh=mesh,
        in_specs=(
            P("hst", "tp"),
            P(None, "hst", None),
            P(),
            P("hst", "tp"),
            P(None, "hst", None),
            P("tp", "hst"),
        ),
        out_specs=(P("hst", "tp"), P(None, "hst")),
        check_vma=False,
    )
```

time: 42.7 us -> 40.1 us (0.939)
  Pallas kernels: 41.9 us -> 39.3 us
    pallas_call x1, Pallas kernels: 41 us -> 38.4 us  [per_device(): pl.pallas_call(kernel, out_shape=(pltpu.VMEM((ROWS, HEADS * HD), bf16), p...]
where the time goes in v5:
time: 40.1 us; the launch traced here: 40 us
  Pallas kernels  39.3 us (98%)
  between operations  0.64 us (2%)
    pallas_call x1, Pallas kernels, per_device(): pl.pallas_call(kernel, out_shape=(pltpu.VMEM((ROWS, HEADS * HD), bf16), p...  38.4 us
    pallas_call x1, Pallas kernels, per_device(): pl.pallas_call(save, out_shape=(jax.ShapeDtypeStruct((ROWS, HEADS * HD),...  0.9 us

profile of v5, /device:TPU:1, one launch (start us, length us, event | category | flops | bytes accessed | tf_op | source)
XLA Modules:
  0.0 40.0 jit_solution(1297103647086005284)
XLA Ops:
  0.6 38.4 %shard_map.77 = (bf16[768,512]{1,0:T(8,128)(2,1)S(1)}, bf16[64,256]{1,0:T(8,128)(2,1)S(1)}) custom-call(s32[32]{0:T(128)} %lengths_hbm.1, bf16[768,512]{1,0:T(8,128)(2,1)} %ctx_q.1, bf16[2,768,1024]{2,1,0:T(8,128)(2,1)} %ctx_kv.1, bf16[2,512]{1,0:T(2,128)(2,1)} %query_q.1, bf16[2,2,1024]{2,1,0:T(2,128)(2,1)} %query_kv.1, bf16[512,256]{1,0:T(8,128)(2,1)} %out_weight.1), custom_call_target="tpu_custom_call" | custom-call | tf_op jit(solution)/shard_map/pallas_call | solution.py:516
  39.0 0.9 %shard_map.78 = (bf16[768,512]{1,0:T(8,128)(2,1)}, bf16[64,256]{1,0:T(8,128)(2,1)}) custom-call(bf16[768,512]{1,0:T(8,128)(2,1)S(1)} %get-tuple-element.4.ctx_in, bf16[64,256]{1,0:T(8,128)(2,1)S(1)} %get-tuple-element.5.query_in), custom_call_target="tpu_custom_call" | custom-call | tf_op jit(solution)/shard_map/pallas_call | solution.py:557

commit v6 on v5

--- a/solution.py
+++ b/solution.py
@@ -30,9 +30,9 @@
 GROUPS = ((0, 5), (5, 11), (11, 16))
 A_SEMS = (0, 9, 10)
 TILES = 8
-ADDERS = (10, 11, 12, 13, 14, 15, 1, 2)
-HIGH = 10
-LOW = 1
+ADDERS = (11, 12, 13, 14, 15, 0, 1, 2)
+HIGH = 11
+LOW = 0
 
 
 def dot_t(a, b):
@@ -201,7 +201,7 @@
             recv_sem.at[A_SEMS[group]], device_id=at_hst(d), device_id_type=MESH,
         ).start()
 
-    for group in (2, 1, 0):
+    for group in (2, 0, 1):
         for k in reversed(range(*GROUPS[group])):
             if k:
                 send_a(chip_at(*SLOTS[k]) * 2, k, group)
@@ -244,7 +244,7 @@
         ).start()
 
     load_cq.wait()
-    first = jnp.where(me == 0, 0, 2)
+    first = jnp.where(me == 0, 0, 1)
     pl.loop(0, first)(own_head)
 
     def landed(ref, n, sem):
@@ -308,7 +308,7 @@
     def _():
         got_b[pl.ds(me, 1)] = sent_b[CHIPS - 1 : CHIPS]
 
-    pl.loop(first, HEADS)(own_head)
+    pl.loop(first, 3)(own_head)
     opposite = chip_at(2, 2)
 
     def send_c(d):
@@ -338,6 +338,8 @@
             send_c(c * 2)
         send_c(mate)
 
+    own_head(3)
+
     @pl.when(me > 0)
     def _():
         pltpu.make_async_copy(
@@ -366,7 +368,7 @@
     def _():
         landed(att, CHIPS - 1, recv_sem.at[5])
 
-    rows_f[...] = att[...].astype(jnp.float32).reshape(HST * 8, HD)
+    rows_f[0 : HST * 8] = att[...].astype(jnp.float32).reshape(HST * 8, HD)
     wide = jnp.concatenate(
         [rows_f[pl.ds(h, QN, stride=HEADS), :] for h in range(HEADS)], axis=1
     ).astype(jnp.bfloat16)
@@ -398,25 +400,29 @@
         def _():
             got_d[1, pl.ds(z, 1)] = part[pl.ds(t, 1)]
 
-    @pl.when(me > 0)
-    def _():
-        pltpu.make_async_copy(
-            anchor.at[0, pl.ds(0, ROWS - PIECE)], anchor.at[0, pl.ds(0, ROWS - PIECE)], recv_sem.at[2]
-        ).wait()
-
-    @pl.when(me > 1)
-    def _():
-        pltpu.make_async_remote_copy(
-            anchor.at[core], anchor.at[core], send_sem.at[4], recv_sem.at[3],
-            device_id=at_hst(mate), device_id_type=MESH,
-        ).start()
-
-    @pl.when(me > 0)
-    def _():
-        pltpu.make_async_copy(anchor.at[0], anchor.at[0], recv_sem.at[3]).wait()
-
-    early = jnp.where(z < TP // 2, HEADS, 0)
-    pl.loop(0, early)(finish_head)
+    def finish():
+        @pl.when(me > 0)
+        def _():
+            pltpu.make_async_copy(
+                anchor.at[0, pl.ds(0, ROWS - PIECE)], anchor.at[0, pl.ds(0, ROWS - PIECE)], recv_sem.at[2]
+            ).wait()
+
+        @pl.when(me > 1)
+        def _():
+            pltpu.make_async_remote_copy(
+                anchor.at[core], anchor.at[core], send_sem.at[4], recv_sem.at[3],
+                device_id=at_hst(mate), device_id_type=MESH,
+            ).start()
+
+        @pl.when(me > 0)
+        def _():
+            pltpu.make_async_copy(anchor.at[0], anchor.at[0], recv_sem.at[3]).wait()
+
+        pl.loop(0, HEADS)(finish_head)
+
+    @pl.when(z < TP // 2)
+    def _():
+        finish()
 
     def send_e(src, d, core_to):
         pltpu.make_async_remote_copy(
@@ -441,7 +447,9 @@
         for d in range(TP):
             send_e(summed, d, 0)
 
-    pl.loop(early, HEADS)(finish_head)
+    @pl.when(z >= TP // 2)
+    def _():
+        finish()
 
     @pl.when(adds)
     def _():
@@ -499,10 +507,10 @@
 
 
 def save(ctx_in, query_in, ctx_out, query_out, sems):
-    copies = (
-        pltpu.make_async_copy(ctx_in, ctx_out, sems.at[0]),
-        pltpu.make_async_copy(query_in, query_out, sems.at[1]),
-    )
+    copies = [pltpu.make_async_copy(query_in, query_out, sems.at[6])]
+    for i in range(6):
+        rows = pl.ds(i * HD, HD)
+        copies.append(pltpu.make_async_copy(ctx_in.at[rows], ctx_out.at[rows], sems.at[i]))
     for copy in copies:
         copy.start()
     for copy in copies:
@@ -534,7 +542,7 @@
             pltpu.VMEM((HEADS, ROWS, HD), f32),
             pltpu.VMEM((HEADS, ROWS, HD), f32),
             pltpu.VMEM((HST, 8, HD), bf16),
-            pltpu.VMEM((HST * 8, HD), f32),
+            pltpu.VMEM((HST * 8 + 8, HD), f32),
             pltpu.VMEM((CHIPS, 32, HD), bf16),
             pltpu.VMEM((HST, 32, HD), bf16),
             pltpu.VMEM((CHIPS, 16, HD), bf16),
@@ -562,7 +570,7 @@
         ),
         in_specs=[any_space] * 2,
         out_specs=(any_space, any_space),
-        scratch_shapes=[pltpu.SemaphoreType.DMA((2,))],
+        scratch_shapes=[pltpu.SemaphoreType.DMA((7,))],
     )(*(pltpu.with_memory_space_constraint(a, pltpu.VMEM) for a in outs))
 
 

time: 40.1 us -> 39.7 us (0.990)
  Pallas kernels: 39.3 us -> 38.8 us
    pallas_call x1, Pallas kernels: 38.4 us -> 37.9 us  [per_device(): pl.pallas_call(kernel, out_shape=(pltpu.VMEM((ROWS, HEADS * HD), bf16), p...]
where the time goes in v6:
time: 39.7 us; the launch traced here: 39.4 us
  Pallas kernels  38.8 us (98%)
  between operations  0.64 us (2%)
    pallas_call x1, Pallas kernels, per_device(): pl.pallas_call(kernel, out_shape=(pltpu.VMEM((ROWS, HEADS * HD), bf16), p...  37.9 us
    pallas_call x1, Pallas kernels, per_device(): pl.pallas_call(save, out_shape=(jax.ShapeDtypeStruct((ROWS, HEADS * HD),...  0.94 us

profile of v6, /device:TPU:1, one launch (start us, length us, event | category | flops | bytes accessed | tf_op | source)
XLA Modules:
  0.0 39.4 jit_solution(12686197921824702531)
XLA Ops:
  0.6 37.9 %shard_map.77 = (bf16[768,512]{1,0:T(8,128)(2,1)S(1)}, bf16[64,256]{1,0:T(8,128)(2,1)S(1)}) custom-call(s32[32]{0:T(128)} %lengths_hbm.1, bf16[768,512]{1,0:T(8,128)(2,1)} %ctx_q.1, bf16[2,768,1024]{2,1,0:T(8,128)(2,1)} %ctx_kv.1, bf16[2,512]{1,0:T(2,128)(2,1)} %query_q.1, bf16[2,2,1024]{2,1,0:T(2,128)(2,1)} %query_kv.1, bf16[512,256]{1,0:T(8,128)(2,1)} %out_weight.1), custom_call_target="tpu_custom_call" | custom-call | tf_op jit(solution)/shard_map/pallas_call | solution.py:524
  38.5 0.9 %shard_map.78 = (bf16[768,512]{1,0:T(8,128)(2,1)}, bf16[64,256]{1,0:T(8,128)(2,1)}) custom-call(bf16[768,512]{1,0:T(8,128)(2,1)S(1)} %get-tuple-element.4.ctx_in, bf16[64,256]{1,0:T(8,128)(2,1)S(1)} %get-tuple-element.5.query_in), custom_call_target="tpu_custom_call" | custom-call | tf_op jit(solution)/shard_map/pallas_call | solution.py:565
